TPU v7x, 32 devices: a whole 2x2x4 slice. The times are simulated.
32 devices in a mesh: grp: 2 (over x), ep: 16 (over z, y, core).
Axes of the slice: x: 2, y: 2, z: 4, core: 2. Of those that a mesh axis runs over, the one named last changes fastest.
Arguments:
- page_key_value_codes: bfloat16 [1024, 32, 1024], P(('grp', 'ep')), parts along dimension 0, may hold values from -6 to 6
- page_key_scales: bfloat16 [1024, 2], P(('grp', 'ep')), parts along dimension 0, may hold values from 0.5 to 2
- page_value_scales: bfloat16 [1024, 2], P(('grp', 'ep')), parts along dimension 0, may hold values from 4 to 32
- block_table: int32 [32, 32], P('grp', 'ep'), parts along dimension 0, may hold values from 0 to 31, as said below
- prompt_lengths: int32 [32], P('grp'), parts along dimension 0, may hold values from 512 to 1024, as said below
- decode_owner: int32 [32], P('grp'), parts along dimension 0, may hold values from 0 to 15, each once
- prefill_states: bfloat16 [32, 32, 128, 128], P('grp', 'ep'), parts along dimension 0, may hold values from -48 to 48
- att_query: bfloat16 [512, 4, 2048], P(('grp', 'ep')), parts along dimension 0, may hold values from -144 to 144
- att_gate: bfloat16 [512, 4, 2048], P(('grp', 'ep')), parts along dimension 0, may hold values from -6 to 6
- draft_keys_values: bfloat16 [512, 4, 1024], P(('grp', 'ep')), parts along dimension 0, may hold values from -24 to 24
- out_weight: bfloat16 [2048, 2048], replicated, may hold values from -0.125 to 0.125
- residual: bfloat16 [512, 4, 2048], P(('grp', 'ep')), parts along dimension 0, may hold values from -6 to 6
- norm_gain: bfloat16 [2048], replicated, may hold values from 0.099609375 to 1.8984375
- router_weight: bfloat16 [2048, 16], replicated, may hold values from -0.125 to 0.125
- expert_routes: int32 [512, 4, 8], P(('grp', 'ep')), parts along dimension 0, may hold values from 0 to 15, all different within a row; in each aligned block of 64 rows (0 to 63, 64 to 127, ..., all dimensions but the last counted through in order) at most 32 rows name the same one
- gate_weight: bfloat16 [16, 2048, 512], P('ep'), may hold values from -0.125 to 0.125
- up_weight: bfloat16 [16, 2048, 512], P('ep'), may hold values from -0.125 to 0.125
- down_weight: bfloat16 [16, 512, 2048], P('ep'), may hold values from -0.25 to 0.25
- gdn_qk: bfloat16 [512, 4, 4096], P(('grp', 'ep')), parts along dimension 0, may hold values from -8.4 to 8.4
- gdn_v: bfloat16 [512, 4, 4096], P(('grp', 'ep')), parts along dimension 0, may hold values from -12 to 12
- gdn_decay: float32 [512, 4, 32], P(('grp', 'ep')), parts along dimension 0, may hold values from 0.5 to 1
- gdn_beta: float32 [512, 4, 32], P(('grp', 'ep')), parts along dimension 0, may hold values from 0.1 to 1
Outputs:
- attn_mix: bfloat16 [512, 4, 2048], P(('grp', 'ep')), parts along dimension 0
- moe_out: bfloat16 [512, 4, 2048], P(('grp', 'ep')), parts along dimension 0
- gdn_out: bfloat16 [512, 4, 4096], P(('grp', 'ep')), parts along dimension 0
There are 2 independent parts, one for each index of `grp`. A program takes and returns all parts, laid end to end along the dimension named above; an argument that names none is the same for every part. Nothing has to cross between parts.
Inputs may be any that keep to these rules, and one draw needn't show every extreme that they name: `block_table`: the 2 columns of one ep device name each of that device's 16 * 2 pages once. `prompt_lengths`: some prompt is 1024 long. `decode_owner`: each device decodes exactly one prompt. `expert_routes`: the 8 experts of one row and draft differ; among the 64 row-draft pairs of one decode device no expert is named more than 32 times, and one is named exactly 32 times in some devices' rows.
All inputs are finite; a program needn't handle non-finite values.
Results may differ from a plain program's by a relative error of at most 0.011.
Values may be sent and summed in bfloat16 or wider, within the bound.
A program may use at most 128 MiB of HBM per device.

v0:
```python
import jax
import jax.numpy as jnp
from jax import lax
from jax.sharding import PartitionSpec as P

QUERY_HEADS = 8
KEY_VALUE_HEADS = 2
HEAD_SIZE = 256
DK = 128
TOPK = 8
CAP = 32
PAGE_POSITIONS = 32


norm_eps = 1e-06
masked_score = -1e30


def attend_prompt(
    rows_of_queries,
    gate_rows,
    fresh_keys_values,
    codes_by_row,
    scale_of_key,
    scale_of_value,
    length,
):
    beam_total = rows_of_queries.shape[0]
    draft_tokens = rows_of_queries.shape[1]
    query_groups = QUERY_HEADS // KEY_VALUE_HEADS
    span_length = codes_by_row.shape[0]
    query_vectors = rows_of_queries.reshape(
        beam_total, draft_tokens, KEY_VALUE_HEADS, query_groups, HEAD_SIZE
    )
    rows_of_keys = codes_by_row[:, : KEY_VALUE_HEADS * HEAD_SIZE].reshape(
        span_length, KEY_VALUE_HEADS, HEAD_SIZE
    )
    rows_of_values = codes_by_row[:, KEY_VALUE_HEADS * HEAD_SIZE :].reshape(
        span_length, KEY_VALUE_HEADS, HEAD_SIZE
    )
    key_pos = jnp.repeat(scale_of_key.astype(jnp.float32), PAGE_POSITIONS, axis=0).T
    value_pos = jnp.repeat(scale_of_value.astype(jnp.float32), PAGE_POSITIONS, axis=0).T
    fresh_keys = fresh_keys_values[:, :, : KEY_VALUE_HEADS * HEAD_SIZE].reshape(
        beam_total, draft_tokens, KEY_VALUE_HEADS, HEAD_SIZE
    )
    fresh_values = fresh_keys_values[:, :, KEY_VALUE_HEADS * HEAD_SIZE :].reshape(
        beam_total, draft_tokens, KEY_VALUE_HEADS, HEAD_SIZE
    )
    factor = HEAD_SIZE ** (-0.5)
    cached = (
        jnp.einsum(
            "btgqd,lgd->btgql", query_vectors, rows_of_keys, preferred_element_type=jnp.float32
        )
        * key_pos[None, None, :, None, :]
        * factor
    )
    live_mask = jnp.arange(span_length, dtype=jnp.int32) < length
    cached = jnp.where(live_mask[None, None, None, None, :], cached, masked_score)
    own_scores = (
        jnp.einsum(
            "btgqd,bsgd->btgqs", query_vectors, fresh_keys, preferred_element_type=jnp.float32
        )
        * factor
    )
    draft_order = jnp.arange(draft_tokens, dtype=jnp.int32)
    causal = draft_order[:, None] >= draft_order[None, :]
    own_scores = jnp.where(causal[None, :, None, None, :], own_scores, masked_score)
    top_score = jnp.maximum(jnp.max(cached, axis=-1), jnp.max(own_scores, axis=-1))[..., None]
    cached_exp = jnp.exp(cached - top_score)
    own_exp = jnp.exp(own_scores - top_score)
    total = jnp.sum(cached_exp, axis=-1, keepdims=True) + jnp.sum(own_exp, axis=-1, keepdims=True)
    cached_w = (cached_exp / total * value_pos[None, None, :, None, :]).astype(jnp.bfloat16)
    own_w = (own_exp / total).astype(jnp.bfloat16)
    mixed = jnp.einsum(
        "btgql,lgd->btgqd", cached_w, rows_of_values, preferred_element_type=jnp.float32
    )
    mixed = mixed + jnp.einsum(
        "btgqs,bsgd->btgqd", own_w, fresh_values, preferred_element_type=jnp.float32
    )
    mixed = mixed.reshape(beam_total, draft_tokens, QUERY_HEADS * HEAD_SIZE)
    return (mixed * jax.nn.sigmoid(gate_rows.astype(jnp.float32))).astype(jnp.bfloat16)


def expert_rows(received, gate_w, up_w, down_w):
    model_width = received.shape[-1]
    flat_rows = received.reshape(-1, model_width)
    gate_val = jnp.dot(flat_rows, gate_w, preferred_element_type=jnp.float32)
    up_val = jnp.dot(flat_rows, up_w, preferred_element_type=jnp.float32)
    inner_act = (jax.nn.silu(gate_val) * up_val).astype(jnp.bfloat16)
    produced = jnp.dot(inner_act, down_w, preferred_element_type=jnp.float32).astype(jnp.bfloat16)
    return produced.reshape(received.shape)


def place_slots(routes, row_ids, experts, capacity, fill_row):
    flat_ids = routes.reshape(-1)
    labels = jnp.arange(experts, dtype=jnp.int32)
    matches = (flat_ids[:, None] == labels[None, :]).astype(jnp.int32)
    earlier = jnp.cumsum(matches, axis=0) - matches
    slot_ids = jnp.sum(earlier * matches, axis=1)
    target = flat_ids * capacity + slot_ids
    sources = jnp.repeat(row_ids, routes.shape[1])
    slot_table = jnp.full((experts * capacity,), fill_row, jnp.int32).at[target].set(sources)
    return (target, slot_table)


def normalize(vectors):
    return vectors * lax.rsqrt(jnp.sum(vectors * vectors, axis=-1, keepdims=True) + norm_eps)


def on_device(
    page_key_value_codes,
    page_key_scales,
    page_value_scales,
    block_table,
    prompt_lengths,
    decode_owner,
    prefill_states,
    att_query,
    att_gate,
    draft_keys_values,
    out_weight,
    residual,
    norm_gain,
    router_weight,
    expert_routes,
    gate_weight,
    up_weight,
    down_weight,
    gdn_qk,
    gdn_v,
    gdn_decay,
    gdn_beta,
):
    devices = lax.axis_size("ep")
    device_id = lax.axis_index("ep")
    labels = jnp.arange(devices, dtype=jnp.int32)
    matches = (decode_owner[:, None] == labels[None, :]).astype(jnp.int32)
    inverse = jnp.sum(labels[:, None] * matches, axis=0)
    page_ids = block_table[inverse]
    send_parts = (
        page_key_value_codes[page_ids],
        page_key_scales[page_ids],
        page_value_scales[page_ids],
        prefill_states[inverse],
    )
    codes_input, key_scale_input, value_scale_input, state_input = (
        lax.all_to_all(send_parts[0], "ep", split_axis=0, concat_axis=1, tiled=True),
        lax.all_to_all(send_parts[1], "ep", split_axis=0, concat_axis=1, tiled=True),
        lax.all_to_all(send_parts[2], "ep", split_axis=0, concat_axis=1, tiled=True),
        lax.all_to_all(send_parts[3], "ep", split_axis=0, concat_axis=1, tiled=True),
    )
    prompt_id = inverse[device_id]
    length = prompt_lengths[prompt_id]
    codes_by_row = codes_input.reshape(-1, codes_input.shape[-1])
    scale_of_key = key_scale_input.reshape(-1, KEY_VALUE_HEADS)
    scale_of_value = value_scale_input.reshape(-1, KEY_VALUE_HEADS)
    gated_out = attend_prompt(
        att_query, att_gate, draft_keys_values, codes_by_row, scale_of_key, scale_of_value, length
    )
    beam_total = att_query.shape[0]
    draft_tokens = att_query.shape[1]
    row_count = beam_total * draft_tokens
    attn_mix = jnp.dot(
        gated_out.reshape(row_count, -1), out_weight, preferred_element_type=jnp.float32
    ).astype(jnp.bfloat16)
    hidden = residual.astype(jnp.float32).reshape(row_count, -1) + attn_mix.astype(jnp.float32)
    normed = (
        hidden
        * lax.rsqrt(jnp.mean(hidden * hidden, axis=-1, keepdims=True) + norm_eps)
        * norm_gain.astype(jnp.float32)
    ).astype(jnp.bfloat16)
    logits = jnp.dot(normed, router_weight, preferred_element_type=jnp.float32)
    routes = expert_routes.reshape(row_count, -1)
    mixing = jax.nn.softmax(jnp.take_along_axis(logits, routes, axis=1), axis=-1)
    experts = router_weight.shape[1]
    model_width = normed.shape[1]
    padded = jnp.concatenate([normed, jnp.zeros((1, model_width), jnp.bfloat16)], axis=0)
    all_rows = jnp.arange(row_count, dtype=jnp.int32)
    target, slot_table = place_slots(routes, all_rows, experts, CAP, row_count)
    buffer = padded[slot_table].reshape(experts, CAP, model_width)
    produced = expert_rows(
        lax.all_to_all(buffer, "ep", split_axis=0, concat_axis=0, tiled=True),
        gate_weight[0],
        up_weight[0],
        down_weight[0],
    )
    back_rows = lax.all_to_all(produced, "ep", split_axis=0, concat_axis=0, tiled=True)
    gathered = back_rows.reshape(experts * CAP, model_width)[target].reshape(
        row_count, TOPK, model_width
    )
    moe_rows = jnp.sum(mixing[:, :, None] * gathered.astype(jnp.float32), axis=1)
    moe_out = moe_rows.astype(jnp.bfloat16)
    current_state = state_input[0].astype(jnp.float32)
    head_count = current_state.shape[0]
    half_width = gdn_qk.shape[-1] // 2
    key_heads = half_width // DK
    head_pairs = head_count // key_heads
    qk_values = gdn_qk.astype(jnp.float32)
    query_vec = normalize(
        qk_values[..., :half_width].reshape(beam_total, draft_tokens, key_heads, DK)
    ) * DK ** (-0.5)
    key_vec = normalize(
        qk_values[..., half_width:].reshape(beam_total, draft_tokens, key_heads, DK)
    )
    query_vec = jnp.repeat(query_vec, head_pairs, axis=2)
    key_vec = jnp.repeat(key_vec, head_pairs, axis=2)
    probe_queries = jnp.concatenate([key_vec, query_vec], axis=1)
    cache_images = jnp.einsum(
        "ijr,flij->flir", current_state, probe_queries, precision=lax.Precision.HIGHEST
    )
    inner_prod = jnp.einsum(
        "bthk,bnhk->btnh", key_vec, probe_queries, precision=lax.Precision.HIGHEST
    )
    value_vec = gdn_v.astype(jnp.float32).reshape(beam_total, draft_tokens, head_count, -1)
    outputs = []
    for draft_idx in range(draft_tokens):
        decay_now = gdn_decay[:, draft_idx][:, None, :, None]
        write_rate = gdn_beta[:, draft_idx][:, None, :, None]
        keyed_image = cache_images[:, draft_idx][:, None]
        along_key = inner_prod[:, draft_idx][..., None]
        cache_images = (
            decay_now * cache_images
            + write_rate * (value_vec[:, draft_idx][:, None] - decay_now * keyed_image) * along_key
        )
        outputs.append(cache_images[:, draft_tokens + draft_idx])
    gdn_out = jnp.stack(outputs, axis=1).reshape(beam_total, draft_tokens, -1).astype(jnp.bfloat16)
    return (
        attn_mix.reshape(beam_total, draft_tokens, -1),
        moe_out.reshape(beam_total, draft_tokens, -1),
        gdn_out,
    )


def solution(mesh):
    placed = (
        P(("grp", "ep"), None, None),
        P(("grp", "ep"), None),
        P(("grp", "ep"), None),
        P("grp", "ep"),
        P("grp"),
        P("grp"),
        P("grp", "ep", None, None),
        P(("grp", "ep"), None, None),
        P(("grp", "ep"), None, None),
        P(("grp", "ep"), None, None),
        P(),
        P(("grp", "ep"), None, None),
        P(),
        P(),
        P(("grp", "ep"), None, None),
        P("ep", None, None),
        P("ep", None, None),
        P("ep", None, None),
        P(("grp", "ep"), None, None),
        P(("grp", "ep"), None, None),
        P(("grp", "ep"), None, None),
        P(("grp", "ep"), None, None),
    )
    return jax.shard_map(
        on_device,
        mesh=mesh,
        in_specs=placed,
        out_specs=(
            P(("grp", "ep"), None, None),
            P(("grp", "ep"), None, None),
            P(("grp", "ep"), None, None),
        ),
        check_vma=False,
    )
```

profile of v0, /device:TPU:13, one launch (start us, length us, event | category | flops | bytes accessed | tf_op | source)
XLA Modules:
  0.0 236.7 jit_solution(18052294479282406520)
XLA Ops:
  5.3 6.6 %all-to-all-start.1 = ((bf16[16,2,2]{1,2,0:T(2,128)(2,1)}), bf16[16,2,2]{1,2,0:T(2,128)(2,1)S(1)}, u32[]{:S(2)}, u32[]{:S(2)}) async-start(bf16[16,2,2]{1,2,0:T(2,128)(2,1)} %copy.362), calls=%async_computation.1 | async-start | bytes 16384 | tf_op jit(solution)/shard_map/all_to_all | solution.py:148
  14.0 1.6 all-to-all-done.1
  15.6 6.0 %all-to-all-start.2 = ((bf16[16,2,2]{1,2,0:T(2,128)(2,1)}), bf16[16,2,2]{1,2,0:T(2,128)(2,1)S(1)}, u32[]{:S(2)}, u32[]{:S(2)}) async-start(bf16[16,2,2]{1,2,0:T(2,128)(2,1)} %copy.371), calls=%async_computation.2 | async-start | bytes 16384 | tf_op jit(solution)/shard_map/all_to_all | solution.py:149
  21.6 2.0 gather_fusion.1
  23.6 1.7 all-to-all-done.2
  26.0 6.4 %all-to-all-start = ((bf16[16,2,32,1024]{3,2,1,0:T(8,128)(2,1)}), bf16[16,2,32,1024]{3,2,1,0:T(8,128)(2,1)S(1)}, u32[]{:S(2)}, u32[]{:S(2)}) async-start(bf16[16,2,32,1024]{3,2,1,0:T(8,128)(2,1)} %bitcast.161), calls=%async_computation | async-start | bytes 4194304 | tf_op jit(solution)/shard_map/all_to_all | solution.py:147
  34.5 1.7 gather_fusion.6
  43.0 2.4 %scatter_custom_fusion = s32[512]{0:T(512)S(1)} fusion(s32[512]{0:T(512)S(1)} %bitcast.192, s32[512]{0:T(512)S(1)} %reshape.462, s32[]{:T(128)} %constant.14.clone.1), kind=kCustom, calls=%fused_computation.108 | custom fusion | bytes 2052 | tf_op jit(solution)/shard_map/scatter | solution.py:102
  47.1 32.7 %all-to-all-done = bf16[16,2,32,1024]{3,2,1,0:T(8,128)(2,1)S(1)} async-done(((bf16[16,2,32,1024]{3,2,1,0:T(8,128)(2,1)}), bf16[16,2,32,1024]{3,2,1,0:T(8,128)(2,1)S(1)}, u32[]{:S(2)}, u32[]{:S(2)}) %all-to-all-start) | async-done | bytes 2097184 | tf_op jit(solution)/shard_map/all_to_all | solution.py:147
  79.8 4.9 %all-to-all-start.5 = ((bf16[16,2,128,128]{3,2,1,0:T(8,128)(2,1)}), bf16[16,2,128,128]{3,2,1,0:T(8,128)(2,1)}, u32[]{:S(2)}, u32[]{:S(2)}) async-start(bf16[16,2,128,128]{3,2,1,0:T(8,128)(2,1)} %gather_fusion.6), calls=%async_computation.5 | async-start | bytes 2097152 | tf_op jit(solution)/shard_map/all_to_all | solution.py:150
  84.7 1.5 fusion.52
  86.2 1.5 copy.357
  87.7 1.9 bitcast_reduce_fusion
  89.7 2.1 fusion.9
  96.9 5.1 %multiply_reduce_fusion.2 = (f32[64]{0:T(128)S(1)}, bf16[64,2048]{1,0:T(8,128)(2,1)S(1)}) fusion(f32[64,2048]{1,0:T(8,128)S(1)} %reshape.392, bf16[64,2048]{1,0:T(8,128)(2,1)S(1)} %reshape.371, bf16[2048,2048]{1,0:T(8,128)(2,1)} %param.32), kind=kOutput, calls=%fused_computation.47 | convolution fusion | flops 537526208 | bytes 9437440 | tf_op jit(solution)/shard_map/dot_general | solution.py:163
  102.7 3.3 %gather_fusion.4 = bf16[512,2048]{1,0:T(8,128)(2,1)} fusion(bf16[65,2048]{1,0:T(8,128)(2,1)S(1)} %concatenate.6, s32[1024]{0:T(1024)S(1)} %pad_clamp_fusion.1), kind=kCustom, calls=%fused_computation.4 | custom fusion | bytes 4196352 | tf_op jit(solution)/shard_map/gather | solution.py:180
  106.0 3.7 %all-to-all-done.5 = bf16[16,2,128,128]{3,2,1,0:T(8,128)(2,1)} async-done(((bf16[16,2,128,128]{3,2,1,0:T(8,128)(2,1)}), bf16[16,2,128,128]{3,2,1,0:T(8,128)(2,1)}, u32[]{:S(2)}, u32[]{:S(2)}) %all-to-all-start.5) | async-done | bytes 1048608 | tf_op jit(solution)/shard_map/all_to_all | solution.py:150
  109.6 5.1 %all-to-all-start.3 = ((bf16[16,32,2048]{2,1,0:T(8,128)(2,1)}), bf16[16,32,2048]{2,1,0:T(8,128)(2,1)}, u32[]{:S(2)}, u32[]{:S(2)}) async-start(bf16[16,32,2048]{2,1,0:T(8,128)(2,1)} %bitcast.30), calls=%async_computation.3 | async-start | bytes 4194304 | tf_op jit(solution)/shard_map/all_to_all | solution.py:182
  119.0 3.7 %fusion.10 = f32[16,4,8,32]{2,1,3,0:T(4,128)S(1)} fusion(f32[16,4,32,128]{3,1,0,2:T(4,128)S(1)} %bitcast.156, f32[16,4,32,128]{3,1,0,2:T(4,128)S(1)} %bitcast.158), kind=kOutput, calls=%fused_computation.31 | convolution fusion | flops 25690112 | bytes 2162688 | tf_op jit(solution)/shard_map/bthk,bnhk->btnh/dot_general | solution.py:211
  129.4 2.9 %convolution_bitcast_fusion = f32[16,8,32,128]{3,1,0,2:T(8,128)S(1)} fusion(bf16[32,128,128,1]{2,1,3,0:T(8,128)(2,1)} %bitcast.43, f32[16,4,32,128]{3,1,0,2:T(4,128)} %bitcast.159, f32[16,4,32,128]{3,1,0,2:T(4,128)S(1)} %bitcast.157), kind=kOutput, calls=%fused_computation.30 | convolution fusion | flops 805830656 | bytes 5242880 | tf_op jit(solution)/shard_map/ijr,flij->flir/dot_general | solution.py:208
  132.3 29.9 %all-to-all-done.3 = bf16[16,32,2048]{2,1,0:T(8,128)(2,1)} async-done(((bf16[16,32,2048]{2,1,0:T(8,128)(2,1)}), bf16[16,32,2048]{2,1,0:T(8,128)(2,1)}, u32[]{:S(2)}, u32[]{:S(2)}) %all-to-all-start.3) | async-done | bytes 2097184 | tf_op jit(solution)/shard_map/all_to_all | solution.py:182
  162.2 3.5 %fusion.4 = f32[512,512]{1,0:T(8,128)S(1)} fusion(bf16[512,2048]{1,0:T(8,128)(2,1)} %bitcast.31, bf16[1,2048,512]{2,1,0:T(8,128)(2,1)} %param.37), kind=kOutput, calls=%fused_computation.17 | convolution fusion | flops 1073741824 | bytes 5242880 | tf_op jit(solution)/shard_map/dot_general | solution.py:87
  165.7 6.9 %convolution_convert_fusion = bf16[512,2048]{1,0:T(8,128)(2,1)} fusion(bf16[1,512,2048]{2,1,0:T(8,128)(2,1)} %param.39, bf16[512,2048]{1,0:T(8,128)(2,1)} %bitcast.31, bf16[1,2048,512]{2,1,0:T(8,128)(2,1)} %param.38, f32[512,512]{1,0:T(8,128)S(1)} %fusion.4), kind=kOutput, calls=%fused_computation.11 | convolution fusion | flops 2150105088 | bytes 9437184 | tf_op jit(solution)/shard_map/dot_general | solution.py:90
  172.6 5.0 %all-to-all-start.4 = ((bf16[16,32,2048]{2,1,0:T(8,128)(2,1)}), bf16[16,32,2048]{2,1,0:T(8,128)(2,1)}, u32[]{:S(2)}, u32[]{:S(2)}) async-start(bf16[16,32,2048]{2,1,0:T(8,128)(2,1)} %bitcast.167), calls=%async_computation.4 | async-start | bytes 4194304 | tf_op jit(solution)/shard_map/all_to_all | solution.py:187
  179.0 1.4 multiply_add_fusion.2
  182.0 2.5 %multiply_add_fusion.1 = f32[16,8,32,128]{3,1,0,2:T(8,128)S(1)} fusion(f32[16,8,32]{1,0,2:T(8,128)S(1)} %copy-done.6, f32[16,32,128]{2,0,1:T(8,128)S(1)} %bitcast.165, f32[16,32]{0,1:T(8,128)S(1)} %copy.405, f32[16,8,32]{1,0,2:T(8,128)S(1)} %copy.404, f32[16,32,128]{2,0,1:T(8,128)S(1)} %bitcast.163, f32[16,8,32,128]{3,1,0,2:T(8,128)S(1)} %convolution_bitcast_fusion, ...), kind=kLoop, calls=%fused_computation.25 | loop fusion | flops 3145728 | bytes 4755456 | tf_op jit(solution)/shard_map/add | solution.py:222
  186.1 3.6 %multiply_add_fusion = f32[16,8,32,128]{3,1,0,2:T(8,128)S(1)} fusion(f32[16,8,32]{1,0,2:T(8,128)S(1)} %copy-done.12, f32[16,32,128]{2,0,1:T(8,128)S(1)} %bitcast.170, f32[16,32]{0,1:T(8,128)S(1)} %copy.410, f32[16,8,32]{1,0,2:T(8,128)S(1)} %copy-done.6, f32[16,32,128]{2,0,1:T(8,128)S(1)} %bitcast.166, f32[16,32]{0,1:T(8,128)S(1)} %copy.405, ...), kind=kLoop, calls=%fused_computation.24 | loop fusion | flops 4718592 | bytes 5036032 | tf_op jit(solution)/shard_map/add | solution.py:222
  192.6 2.0 copy_bitcast_fusion
  194.8 3.9 %gather_fusion.7 = f32[512]{0:T(512)S(1)} fusion(f32[64,16]{0,1:T(8,128)S(1)} %fusion.60, s32[512]{0:T(512)S(1)} %reshape.452), kind=kCustom, calls=%fused_computation.7 | custom fusion | bytes 8192 | tf_op jit(solution)/shard_map/jit(take_along_axis)/gather | solution.py:174
  200.3 24.8 %all-to-all-done.4 = bf16[16,32,2048]{2,1,0:T(8,128)(2,1)} async-done(((bf16[16,32,2048]{2,1,0:T(8,128)(2,1)}), bf16[16,32,2048]{2,1,0:T(8,128)(2,1)}, u32[]{:S(2)}, u32[]{:S(2)}) %all-to-all-start.4) | async-done | bytes 2097184 | tf_op jit(solution)/shard_map/all_to_all | solution.py:187
  225.2 7.2 %gather_fusion.5 = bf16[512,2048]{1,0:T(8,128)(2,1)} fusion(bf16[512,2048]{1,0:T(8,128)(2,1)} %bitcast.36, s32[1024]{0:T(1024)S(1)} %pad_clamp_fusion), kind=kCustom, calls=%fused_computation.5 | custom fusion | bytes 4196352 | tf_op jit(solution)/shard_map/gather | solution.py:188
  232.4 3.4 %fusion = bf16[64,2048]{1,0:T(8,128)(2,1)S(1)} fusion(bf16[512,2048]{1,0:T(8,128)(2,1)} %gather_fusion.5, f32[64,8]{1,0:T(8,128)S(1)} %copy.390), kind=kLoop, calls=%fused_computation.10 | loop fusion | flops 3014656 | bytes 2361344 | tf_op jit(solution)/shard_map/reduce_sum | solution.py:191
  (191 shorter events, 42.2 us)
Async XLA Ops:
  0.6 21.0 %copy-start = (bf16[32,32,1024]{2,1,0:T(8,128)(2,1)S(1)}, bf16[32,32,1024]{2,1,0:T(8,128)(2,1)}, u32[]{:S(2)}) copy-start(bf16[32,32,1024]{2,1,0:T(8,128)(2,1)} %param.22) | copy-start | bytes 6291460
  5.3 10.3 %all-to-all-start.1 = ((bf16[16,2,2]{1,2,0:T(2,128)(2,1)}), bf16[16,2,2]{1,2,0:T(2,128)(2,1)S(1)}, u32[]{:S(2)}, u32[]{:S(2)}) async-start(bf16[16,2,2]{1,2,0:T(2,128)(2,1)} %copy.362), calls=%async_computation.1 | async-start | bytes 16384 | tf_op jit(solution)/shard_map/all_to_all | solution.py:148
  15.6 9.8 %all-to-all-start.2 = ((bf16[16,2,2]{1,2,0:T(2,128)(2,1)}), bf16[16,2,2]{1,2,0:T(2,128)(2,1)S(1)}, u32[]{:S(2)}, u32[]{:S(2)}) async-start(bf16[16,2,2]{1,2,0:T(2,128)(2,1)} %copy.371), calls=%async_computation.2 | async-start | bytes 16384 | tf_op jit(solution)/shard_map/all_to_all | solution.py:149
  26.0 8.3 %copy-start.23 = (s32[16,4,8]{0,2,1:T(8,128)S(1)}, s32[16,4,8]{0,2,1:T(8,128)}, u32[]{:S(2)}) copy-start(s32[16,4,8]{0,2,1:T(8,128)} %param.36) | copy-start | bytes 6148
  26.0 8.6 %copy-start.11 = (bf16[16,2,128,128]{3,2,1,0:T(8,128)(2,1)S(1)}, bf16[16,2,128,128]{3,2,1,0:T(8,128)(2,1)}, u32[]{:S(2)}) copy-start(bf16[16,2,128,128]{3,2,1,0:T(8,128)(2,1)} %param.28) | copy-start | bytes 3145732
  26.0 53.8 %all-to-all-start = ((bf16[16,2,32,1024]{3,2,1,0:T(8,128)(2,1)}), bf16[16,2,32,1024]{3,2,1,0:T(8,128)(2,1)S(1)}, u32[]{:S(2)}, u32[]{:S(2)}) async-start(bf16[16,2,32,1024]{3,2,1,0:T(8,128)(2,1)} %bitcast.161), calls=%async_computation | async-start | bytes 4194304 | tf_op jit(solution)/shard_map/all_to_all | solution.py:147
  34.5 5.3 %copy-start.19 = (bf16[16,4,2048]{2,1,0:T(4,128)(2,1)S(1)}, bf16[16,4,2048]{2,1,0:T(4,128)(2,1)}, u32[]{:S(2)}) copy-start(bf16[16,4,2048]{2,1,0:T(4,128)(2,1)} %param.33) | copy-start | bytes 786436
  36.2 3.7 %copy-start.31 = (bf16[2048]{0:T(1024)(128)(2,1)S(1)}, bf16[2048]{0:T(1024)(128)(2,1)}, u32[]{:S(2)}) copy-start(bf16[2048]{0:T(1024)(128)(2,1)} %param.34) | copy-start | bytes 12292
  36.2 6.1 %copy-start.32 = (s32[16]{0:T(128)S(1)}, s32[16]{0:T(128)}, u32[]{:S(2)}) copy-start(s32[16]{0:T(128)} %param.26) | copy-start | bytes 196
  36.2 10.4 %copy-start.30 = (bf16[16,2,2]{1,2,0:T(2,128)(2,1)S(1)}, bf16[16,2,2]{1,2,0:T(2,128)(2,1)}, u32[]{:S(2)}) copy-start(bf16[16,2,2]{1,2,0:T(2,128)(2,1)} %copy-done.29) | copy-start | bytes 388
  37.4 2.3 copy-start.20
  79.8 29.9 %all-to-all-start.5 = ((bf16[16,2,128,128]{3,2,1,0:T(8,128)(2,1)}), bf16[16,2,128,128]{3,2,1,0:T(8,128)(2,1)}, u32[]{:S(2)}, u32[]{:S(2)}) async-start(bf16[16,2,128,128]{3,2,1,0:T(8,128)(2,1)} %gather_fusion.6), calls=%async_computation.5 | async-start | bytes 2097152 | tf_op jit(solution)/shard_map/all_to_all | solution.py:150
  86.2 1.5 copy-start.21
  89.6 2.8 %copy-start.3 = (bf16[1024,512]{1,0:T(8,128)(2,1)S(1)}, bf16[1024,512]{1,0:T(8,128)(2,1)}, u32[]{:S(2)}) copy-start(bf16[1024,512]{1,0:T(8,128)(2,1)} %get-tuple-element.22) | copy-start | bytes 3145732
  92.9 1.6 copy-start.9
  102.7 3.3 %copy-start.7 = (bf16[64,2048]{1,0:T(8,128)(2,1)}, bf16[64,2048]{1,0:T(8,128)(2,1)S(1)}, u32[]{:S(2)}) copy-start(bf16[64,2048]{1,0:T(8,128)(2,1)S(1)} %multiply_convert_fusion.2) | copy-start | bytes 786436
  109.6 5.1 %copy-start.10 = (bf16[16,4,4096]{2,1,0:T(4,128)(2,1)S(1)}, bf16[16,4,4096]{2,1,0:T(4,128)(2,1)}, u32[]{:S(2)}) copy-start(bf16[16,4,4096]{2,1,0:T(4,128)(2,1)} %param.40) | copy-start | bytes 1572868
  109.6 52.6 %all-to-all-start.3 = ((bf16[16,32,2048]{2,1,0:T(8,128)(2,1)}), bf16[16,32,2048]{2,1,0:T(8,128)(2,1)}, u32[]{:S(2)}, u32[]{:S(2)}) async-start(bf16[16,32,2048]{2,1,0:T(8,128)(2,1)} %bitcast.30), calls=%async_computation.3 | async-start | bytes 4194304 | tf_op jit(solution)/shard_map/all_to_all | solution.py:182
  172.6 5.1 %copy-start.17 = (f32[16,1,32,128]{3,2,1,0:T(8,128)S(1)}, f32[16,1,32,128]{3,2,1,0:T(8,128)}, u32[]{:S(2)}) copy-start(f32[16,1,32,128]{3,2,1,0:T(8,128)} %get-tuple-element.26) | copy-start | bytes 786436
  172.6 52.6 %all-to-all-start.4 = ((bf16[16,32,2048]{2,1,0:T(8,128)(2,1)}), bf16[16,32,2048]{2,1,0:T(8,128)(2,1)}, u32[]{:S(2)}, u32[]{:S(2)}) async-start(bf16[16,32,2048]{2,1,0:T(8,128)(2,1)} %bitcast.167), calls=%async_computation.4 | async-start | bytes 4194304 | tf_op jit(solution)/shard_map/all_to_all | solution.py:187
  178.9 1.7 copy-start.16
  179.0 1.7 copy-start.24
  179.0 3.0 %copy-start.6 = (f32[16,8,32]{1,0,2:T(8,128)S(1)}, f32[16,8,32]{1,0,2:T(8,128)}, u32[]{:S(2)}) copy-start(f32[16,8,32]{1,0,2:T(8,128)} %copy.409) | copy-start | bytes 49156
  182.0 2.8 %copy-start.15 = (f32[16,1,32,128]{3,2,1,0:T(8,128)S(1)}, f32[16,1,32,128]{3,2,1,0:T(8,128)}, u32[]{:S(2)}) copy-start(f32[16,1,32,128]{3,2,1,0:T(8,128)} %get-tuple-element.24) | copy-start | bytes 786436
  182.0 2.8 %copy-start.25 = (f32[16,32]{0,1:T(8,128)S(1)}, f32[16,32]{0,1:T(8,128)}, u32[]{:S(2)}) copy-start(f32[16,32]{0,1:T(8,128)} %copy.411) | copy-start | bytes 6148
  182.0 4.1 %copy-start.12 = (f32[16,8,32]{1,0,2:T(8,128)S(1)}, f32[16,8,32]{1,0,2:T(8,128)}, u32[]{:S(2)}) copy-start(f32[16,8,32]{1,0,2:T(8,128)} %copy.414) | copy-start | bytes 49156
  186.1 3.9 %copy-start.14 = (f32[16,1,32,128]{3,2,1,0:T(8,128)S(1)}, f32[16,1,32,128]{3,2,1,0:T(8,128)}, u32[]{:S(2)}) copy-start(f32[16,1,32,128]{3,2,1,0:T(8,128)} %get-tuple-element.23) | copy-start | bytes 786436
  186.1 5.2 %copy-start.13 = (f32[16,1,32]{1,0,2:T(8,128)S(1)}, f32[16,1,32]{1,0,2:T(8,128)}, u32[]{:S(2)}) copy-start(f32[16,1,32]{1,0,2:T(8,128)} %copy.475) | copy-start | bytes 6148
  189.7 4.9 %copy-start.8 = (bf16[64,2048]{1,0:T(8,128)(2,1)S(1)}, bf16[64,2048]{1,0:T(8,128)(2,1)}, u32[]{:S(2)}) copy-start(bf16[64,2048]{1,0:T(8,128)(2,1)} %copy-done.7) | copy-start | bytes 786436
  189.7 4.9 %copy-start.26 = (bf16[2048,16]{0,1:T(8,128)(2,1)S(1)}, bf16[2048,16]{0,1:T(8,128)(2,1)}, u32[]{:S(2)}) copy-start(bf16[2048,16]{0,1:T(8,128)(2,1)} %param.35) | copy-start | bytes 196612
  194.8 4.1 %copy-start.5 = (bf16[64,2048]{1,0:T(8,128)(2,1)S(1)}, bf16[64,2048]{1,0:T(8,128)(2,1)}, u32[]{:S(2)}) copy-start(bf16[64,2048]{1,0:T(8,128)(2,1)} %copy-done.4) | copy-start | bytes 786436
  225.2 11.5 %copy-start.1 = (bf16[32,32,1024]{2,1,0:T(8,128)(2,1)S(1)}, bf16[32,32,1024]{2,1,0:T(8,128)(2,1)}, u32[]{:S(2)}) copy-start(bf16[32,32,1024]{2,1,0:T(8,128)(2,1)} %param.22) | copy-start | bytes 6291460
  (7 other events, 6.7 us)
where the time goes:
time: 237 us
  waiting for transfers between devices  94.4 us (40%)
  local copies, waits for them, and re-layouts  52 us (22%)
  starting transfers between devices  33.9 us (14%)
  matrix products  26.7 us (11%)
  other arithmetic  26.2 us (11%)
  between operations  3.45 us (1%)
    all_to_all x1, waiting for transfers between devices, on_device(): lax.all_to_all(send_parts[0], 'ep', split_axis=0, concat_axis=1, tiled=True)  32.7 us
    all_to_all x1, waiting for transfers between devices, on_device(): lax.all_to_all(buffer, 'ep', split_axis=0, concat_axis=0, tiled=True)  29.9 us
    all_to_all x1, waiting for transfers between devices, on_device(): lax.all_to_all(produced, 'ep', split_axis=0, concat_axis=0, tiled=True)  24.8 us
    add x3, other arithmetic, on_device(): decay_now * cache_images  7.52 us
    gather x1, local copies, waits for them, and re-layouts, on_device(): back_rows.reshape(experts * CAP, model_width)[target]  7.25 us
    unnamed x71, local copies, waits for them, and re-layouts  7.03 us
    dot_general x1, matrix products, expert_rows(): jnp.dot(inner_act, down_w, preferred_element_type=jnp.float32)  6.87 us
    all_to_all x1, starting transfers between devices, on_device(): lax.all_to_all(send_parts[1], 'ep', split_axis=0, concat_axis=1, tiled=True)  6.55 us
  transfers between devices with their start and end apart: 6, of which 6 were waited for; matrix products, arithmetic and copies ran while one was open for 31% of the time, Pallas kernels for 0%

commit v1 on v0

--- a/solution.py
+++ b/solution.py
@@ -1,7 +1,14 @@
+import functools
+
 import jax
 import jax.numpy as jnp
 from jax import lax
+from jax.experimental import pallas as pl
+from jax.experimental.pallas import tpu as pltpu
 from jax.sharding import PartitionSpec as P
+
+MESH = pl.DeviceIdType.MESH
+MIX_COLUMNS = 128
 
 QUERY_HEADS = 8
 KEY_VALUE_HEADS = 2
@@ -81,26 +88,145 @@
     return (mixed * jax.nn.sigmoid(gate_rows.astype(jnp.float32))).astype(jnp.bfloat16)
 
 
-def expert_rows(received, gate_w, up_w, down_w):
-    model_width = received.shape[-1]
-    flat_rows = received.reshape(-1, model_width)
-    gate_val = jnp.dot(flat_rows, gate_w, preferred_element_type=jnp.float32)
-    up_val = jnp.dot(flat_rows, up_w, preferred_element_type=jnp.float32)
-    inner_act = (jax.nn.silu(gate_val) * up_val).astype(jnp.bfloat16)
-    produced = jnp.dot(inner_act, down_w, preferred_element_type=jnp.float32).astype(jnp.bfloat16)
-    return produced.reshape(received.shape)
-
-
-def place_slots(routes, row_ids, experts, capacity, fill_row):
-    flat_ids = routes.reshape(-1)
-    labels = jnp.arange(experts, dtype=jnp.int32)
-    matches = (flat_ids[:, None] == labels[None, :]).astype(jnp.int32)
-    earlier = jnp.cumsum(matches, axis=0) - matches
-    slot_ids = jnp.sum(earlier * matches, axis=1)
-    target = flat_ids * capacity + slot_ids
-    sources = jnp.repeat(row_ids, routes.shape[1])
-    slot_table = jnp.full((experts * capacity,), fill_row, jnp.int32).at[target].set(sources)
-    return (target, slot_table)
+def expert_kernel(
+    n, x_ref, gate_ref, up_ref, down_ref, out_ref,
+    rows_in, part, core_in, y_in, z_in,
+    z_send, z_recv, y_send, y_recv, c_send, c_recv,
+    core_send, core_recv, fold_send, fold_recv, last_send, last_recv, own_sem,
+):
+    deep = n // 4
+    width = out_ref.shape[1]
+    count = out_ref.shape[0]
+    me = lax.axis_index("ep")
+    c = lax.rem(me, 2)
+    y = lax.rem(me // 2, 2)
+    z = me // 4
+
+    def at(zz, yy, cc):
+        return (zz * 2 + yy) * 2 + cc
+
+    other = at(z, y, 1 - c)
+    across = at(z, 1 - y, c)
+    up_z = [lax.rem(z + k, deep) for k in range(deep)]
+    down_z = [lax.rem(z + deep - k, deep) for k in range(deep)]
+    peers = [other, across] + [at(up_z[k], y, c) for k in range(1, deep)]
+    barrier = pltpu.get_barrier_semaphore()
+    for peer in peers:
+        pl.semaphore_signal(barrier, inc=1, device_id={"ep": peer}, device_id_type=MESH)
+    pl.semaphore_wait(barrier, len(peers))
+
+    def send(src, dst, s_sem, r_sem, peer):
+        copy = pltpu.make_async_remote_copy(
+            src_ref=src, dst_ref=dst, send_sem=s_sem, recv_sem=r_sem,
+            device_id={"ep": peer}, device_id_type=MESH,
+        )
+        copy.start()
+        return copy
+
+    own = pltpu.make_async_copy(x_ref, rows_in.at[me], own_sem)
+    own.start()
+    z_copies = {}
+    y_copies = {0: send(x_ref, rows_in.at[me], y_send.at[0], y_recv.at[0], across)}
+    for k in range(1, deep):
+        z_copies[k] = send(x_ref, rows_in.at[me], z_send.at[k], z_recv.at[k], at(up_z[k], y, c))
+    c_copies = {(0, 0): send(x_ref, rows_in.at[me], c_send.at[0], c_recv.at[0], other)}
+    core_copies, fold_copies, last_copies = {}, {}, {}
+    lanes = lax.broadcasted_iota(jnp.int32, (4 * count, MIX_COLUMNS), 1)
+    picked = (lanes == me) | (lanes == me + n)
+
+    def stage(k):
+        z_copies[k].wait_recv()
+        block = at(down_z[k], y, c)
+        y_copies[k] = send(rows_in.at[block], rows_in.at[block], y_send.at[k], y_recv.at[k], across)
+        c_copies[k, 0] = send(
+            rows_in.at[block], rows_in.at[block], c_send.at[2 * k], c_recv.at[2 * k], other
+        )
+
+    def fold_y(k):
+        y_here = at(down_z[k], y, c)
+        fold_copies[k].wait_recv()
+        part[y_here] = (
+            part[y_here].astype(jnp.float32) + y_in[k].astype(jnp.float32)
+        ).astype(jnp.bfloat16)
+        if k:
+            last_copies[k] = send(
+                part.at[y_here], z_in.at[k], last_send.at[k], last_recv.at[k], y_here
+            )
+
+    for k in range(deep):
+        y_copies[k].wait_recv()
+        block = at(down_z[k], 1 - y, c)
+        c_copies[k, 1] = send(
+            rows_in.at[block], rows_in.at[block], c_send.at[2 * k + 1], c_recv.at[2 * k + 1], other
+        )
+        if k + 1 < deep:
+            stage(k + 1)
+        if k == 0:
+            own.wait()
+        c_copies[k, 0].wait_recv()
+        c_copies[k, 1].wait_recv()
+        first = pl.multiple_of(down_z[k] * 4, 4)
+        rows = rows_in[pl.ds(first, 4)].reshape(4 * count, -1)
+        mix = jnp.sum(
+            jnp.where(picked, rows[:, width:].astype(jnp.float32), 0.0), axis=1, keepdims=True
+        )
+        rows = rows[:, :width]
+        gate_val = jnp.dot(rows, gate_ref[...], preferred_element_type=jnp.float32)
+        up_val = jnp.dot(rows, up_ref[...], preferred_element_type=jnp.float32)
+        inner = (gate_val * jax.nn.sigmoid(gate_val) * up_val).astype(jnp.bfloat16)
+        made = jnp.dot(inner, down_ref[...], preferred_element_type=jnp.float32)
+        part[pl.ds(first, 4)] = (made * mix).astype(jnp.bfloat16).reshape(4, count, width)
+        for yy in range(2):
+            core_copies[k, yy] = send(
+                part.at[at(down_z[k], yy, 1 - c)], core_in.at[2 * k + yy],
+                core_send.at[2 * k + yy], core_recv.at[2 * k + yy], other,
+            )
+        for yy in range(2):
+            core_copies[k, yy].wait_recv()
+            here = at(down_z[k], yy, c)
+            part[here] = (
+                part[here].astype(jnp.float32) + core_in[2 * k + yy].astype(jnp.float32)
+            ).astype(jnp.bfloat16)
+        fold_copies[k] = send(
+            part.at[at(down_z[k], 1 - y, c)], y_in.at[k], fold_send.at[k], fold_recv.at[k], across
+        )
+        if k:
+            fold_y(k - 1)
+    fold_y(deep - 1)
+    total = part[me].astype(jnp.float32)
+    for k in range(1, deep):
+        last_copies[k].wait_recv()
+        total = total + z_in[k].astype(jnp.float32)
+    out_ref[...] = total.astype(jnp.bfloat16)
+    for group in (z_copies, y_copies, c_copies, core_copies, fold_copies, last_copies):
+        for copy in group.values():
+            copy.wait_send()
+
+
+def routed_experts(packed, gate_w, up_w, down_w, n):
+    count = packed.shape[0]
+    width = down_w.shape[1]
+    deep = n // 4
+    dma = pltpu.SemaphoreType.DMA
+    return pl.pallas_call(
+        functools.partial(expert_kernel, n),
+        out_shape=jax.ShapeDtypeStruct((count, width), jnp.bfloat16),
+        in_specs=[pl.BlockSpec(memory_space=pltpu.VMEM)] * 4,
+        out_specs=pl.BlockSpec(memory_space=pltpu.VMEM),
+        scratch_shapes=[
+            pltpu.VMEM((n, count, packed.shape[1]), jnp.bfloat16),
+            pltpu.VMEM((n, count, width), jnp.bfloat16),
+            pltpu.VMEM((2 * deep, count, width), jnp.bfloat16),
+            pltpu.VMEM((deep, count, width), jnp.bfloat16),
+            pltpu.VMEM((deep, count, width), jnp.bfloat16),
+            dma((deep,)), dma((deep,)), dma((deep,)), dma((deep,)),
+            dma((2 * deep,)), dma((2 * deep,)), dma((2 * deep,)), dma((2 * deep,)),
+            dma((deep,)), dma((deep,)), dma((deep,)), dma((deep,)), dma,
+        ],
+        compiler_params=pltpu.CompilerParams(
+            collective_id=1, has_side_effects=True, vmem_limit_bytes=50 * 1024 * 1024
+        ),
+    )(packed, gate_w, up_w, down_w)
 
 
 def normalize(vectors):
@@ -137,23 +263,27 @@
     matches = (decode_owner[:, None] == labels[None, :]).astype(jnp.int32)
     inverse = jnp.sum(labels[:, None] * matches, axis=0)
     page_ids = block_table[inverse]
-    send_parts = (
-        page_key_value_codes[page_ids],
-        page_key_scales[page_ids],
-        page_value_scales[page_ids],
-        prefill_states[inverse],
-    )
-    codes_input, key_scale_input, value_scale_input, state_input = (
-        lax.all_to_all(send_parts[0], "ep", split_axis=0, concat_axis=1, tiled=True),
-        lax.all_to_all(send_parts[1], "ep", split_axis=0, concat_axis=1, tiled=True),
-        lax.all_to_all(send_parts[2], "ep", split_axis=0, concat_axis=1, tiled=True),
-        lax.all_to_all(send_parts[3], "ep", split_axis=0, concat_axis=1, tiled=True),
+    scales = jnp.concatenate(
+        [page_key_scales[page_ids], page_value_scales[page_ids]], axis=-1
+    ).reshape(devices, 1, -1)
+    states = prefill_states[inverse].reshape(devices, -1, DK)
+    scales = jnp.pad(scales, ((0, 0), (0, 15), (0, DK - scales.shape[2])))
+    with_scales = lax.all_to_all(
+        jnp.concatenate([states, scales], axis=1), "ep", split_axis=0, concat_axis=0, tiled=True
+    )
+    state_rows = states.shape[1]
+    state_input = with_scales[:, :state_rows].reshape(-1, DK, DK)
+    scale_input = with_scales[:, state_rows, : page_ids.shape[1] * 2 * KEY_VALUE_HEADS].reshape(
+        -1, 2 * KEY_VALUE_HEADS
+    )
+    codes_input = lax.all_to_all(
+        page_key_value_codes[page_ids], "ep", split_axis=0, concat_axis=0, tiled=True
     )
     prompt_id = inverse[device_id]
     length = prompt_lengths[prompt_id]
     codes_by_row = codes_input.reshape(-1, codes_input.shape[-1])
-    scale_of_key = key_scale_input.reshape(-1, KEY_VALUE_HEADS)
-    scale_of_value = value_scale_input.reshape(-1, KEY_VALUE_HEADS)
+    scale_of_key = scale_input[:, :KEY_VALUE_HEADS]
+    scale_of_value = scale_input[:, KEY_VALUE_HEADS:]
     gated_out = attend_prompt(
         att_query, att_gate, draft_keys_values, codes_by_row, scale_of_key, scale_of_value, length
     )
@@ -171,26 +301,24 @@
     ).astype(jnp.bfloat16)
     logits = jnp.dot(normed, router_weight, preferred_element_type=jnp.float32)
     routes = expert_routes.reshape(row_count, -1)
-    mixing = jax.nn.softmax(jnp.take_along_axis(logits, routes, axis=1), axis=-1)
     experts = router_weight.shape[1]
-    model_width = normed.shape[1]
-    padded = jnp.concatenate([normed, jnp.zeros((1, model_width), jnp.bfloat16)], axis=0)
-    all_rows = jnp.arange(row_count, dtype=jnp.int32)
-    target, slot_table = place_slots(routes, all_rows, experts, CAP, row_count)
-    buffer = padded[slot_table].reshape(experts, CAP, model_width)
-    produced = expert_rows(
-        lax.all_to_all(buffer, "ep", split_axis=0, concat_axis=0, tiled=True),
-        gate_weight[0],
-        up_weight[0],
-        down_weight[0],
-    )
-    back_rows = lax.all_to_all(produced, "ep", split_axis=0, concat_axis=0, tiled=True)
-    gathered = back_rows.reshape(experts * CAP, model_width)[target].reshape(
-        row_count, TOPK, model_width
-    )
-    moe_rows = jnp.sum(mixing[:, :, None] * gathered.astype(jnp.float32), axis=1)
-    moe_out = moe_rows.astype(jnp.bfloat16)
-    current_state = state_input[0].astype(jnp.float32)
+    named = jnp.any(
+        routes[:, :, None] == jnp.arange(experts, dtype=jnp.int32)[None, None, :], axis=1
+    )
+    mixing = jax.nn.softmax(jnp.where(named, logits, -jnp.inf), axis=-1)
+    coarse = lax.reduce_precision(mixing, 8, 7)
+    fine = mixing - coarse
+    packed = jnp.concatenate(
+        [
+            normed,
+            coarse.astype(jnp.bfloat16),
+            fine.astype(jnp.bfloat16),
+            jnp.zeros((row_count, MIX_COLUMNS - 2 * experts), jnp.bfloat16),
+        ],
+        axis=1,
+    )
+    moe_out = routed_experts(packed, gate_weight[0], up_weight[0], down_weight[0], devices)
+    current_state = state_input.astype(jnp.float32)
     head_count = current_state.shape[0]
     half_width = gdn_qk.shape[-1] // 2
     key_heads = half_width // DK

time: 237 us -> 210 us (0.89)
  the two profiles are of different devices: /device:TPU:13 before, /device:TPU:0 now
where the time goes in v1:
time: 210 us; the launch traced here: 209 us
  Pallas kernels  82.1 us (39%)
  local copies, waits for them, and re-layouts  51.4 us (24%)
  other arithmetic  26 us (12%)
  matrix products  17.9 us (9%)
  waiting for transfers between devices  14.9 us (7%)
  starting transfers between devices  13.5 us (6%)
  between operations  2.96 us (1%)
    pallas_call x1, Pallas kernels, routed_experts(): pl.pallas_call(functools.partial(expert_kernel, n), out_shape=jax.ShapeDt...  82.1 us
    all_to_all x1, waiting for transfers between devices, on_device(): lax.all_to_all(page_key_value_codes[page_ids], 'ep', split_axis=0, concat...  14.9 us
    unnamed x78, local copies, waits for them, and re-layouts  7.87 us
    add x3, other arithmetic, on_device(): decay_now * cache_images  7.5 us
    all_to_all x1, starting transfers between devices, on_device(): lax.all_to_all(jnp.concatenate([states, scales], axis=1), 'ep', split_axi...  7.43 us
    all_to_all x1, starting transfers between devices, on_device(): lax.all_to_all(page_key_value_codes[page_ids], 'ep', split_axis=0, concat...  6.02 us
    mul x4, other arithmetic, on_device(): write_rate * (value_vec[:, draft_idx][:, None] - decay_now * keyed_image)  5.16 us
    dot_general x1, matrix products, on_device(): jnp.dot(gated_out.reshape(row_count, -1), out_weight, preferred_element_t...  5.1 us
  transfers between devices with their start and end apart: 2, of which 1 were waited for; matrix products, arithmetic and copies ran while one was open for 27% of the time, Pallas kernels for 0%

profile of v1, /device:TPU:0, one launch (start us, length us, event | category | flops | bytes accessed | tf_op | source)
XLA Modules:
  0.0 208.7 jit_solution(11541622061812446922)
XLA Ops:
  6.2 2.0 gather_fusion.2
  9.2 7.4 %all-to-all-start.1 = ((bf16[16,272,128]{2,1,0:T(8,128)(2,1)}), bf16[16,272,128]{2,1,0:T(8,128)(2,1)}, u32[]{:S(2)}, u32[]{:S(2)}) async-start(bf16[16,272,128]{2,1,0:T(8,128)(2,1)} %fusion.11), calls=%async_computation.1 | async-start | bytes 2228224 | tf_op jit(solution)/shard_map/all_to_all | solution.py:271
  19.2 2.0 gather_fusion.1
  22.1 2.0 fusion.40
  25.9 1.3 reshape.201
  31.3 3.7 %fusion.5 = f32[16,4,8,32]{2,1,3,0:T(4,128)S(1)} fusion(f32[16,4,32,128]{3,1,0,2:T(4,128)S(1)} %bitcast.110, f32[16,4,32,128]{3,1,0,2:T(4,128)S(1)} %bitcast.112), kind=kOutput, calls=%fused_computation.21 | convolution fusion | flops 25690112 | bytes 2162688 | tf_op jit(solution)/shard_map/bthk,bnhk->btnh/dot_general | solution.py:339
  35.0 1.5 fusion.34
  38.4 2.5 %reshape.260 = f32[16,4,32,128]{3,2,1,0:T(8,128)} reshape(bf16[16,4,4096]{2,1,0:T(4,128)(2,1)} %param.41) | data formatting | bytes 1572864 | tf_op jit(solution)/shard_map/reshape | solution.py:342
  47.7 2.2 %fusion.33 = (f32[16,1,32,128]{3,2,1,0:T(8,128)}, f32[16,1,32,128]{3,2,1,0:T(8,128)}, f32[16,1,32,128]{3,2,1,0:T(8,128)}, f32[16,1,32,128]{3,2,1,0:T(8,128)}) fusion(f32[16,4,32,128]{3,2,1,0:T(8,128)} %reshape.260), kind=kLoop, calls=%fused_computation.87 | loop fusion | bytes 2097152 | tf_op jit(solution)/shard_map/slice | solution.py:351
  49.9 6.0 %all-to-all-start = ((bf16[16,2,32,1024]{3,2,1,0:T(8,128)(2,1)}), bf16[16,2,32,1024]{3,2,1,0:T(8,128)(2,1)}, u32[]{:S(2)}, u32[]{:S(2)}) async-start(bf16[16,2,32,1024]{3,2,1,0:T(8,128)(2,1)} %bitcast.114), calls=%async_computation | async-start | bytes 4194304 | tf_op jit(solution)/shard_map/all_to_all | solution.py:279
  59.4 1.4 copy.423
  62.2 1.4 slice.157
  63.8 1.5 convolution_bitcast_fusion
  65.3 1.3 fusion.21
  66.6 1.4 multiply_add_fusion.2
  68.3 1.3 fusion.22
  69.7 2.5 %multiply_add_fusion.1 = f32[16,8,32,128]{3,1,0,2:T(8,128)S(1)} fusion(f32[16,8,32]{1,0,2:T(8,128)S(1)} %copy-done.5, f32[16,32,128]{2,0,1:T(8,128)S(1)} %bitcast.120, f32[16,32]{0,1:T(8,128)S(1)} %copy.383, f32[16,8,32]{1,0,2:T(8,128)S(1)} %copy.382, f32[16,32,128]{2,0,1:T(8,128)S(1)} %bitcast.116, f32[16,8,32,128]{3,1,0,2:T(8,128)S(1)} %convolution_bitcast_fusion, ...), kind=kLoop, calls=%fused_computation.15 | loop fusion | flops 3145728 | bytes 4755456 | tf_op jit(solution)/shard_map/add | solution.py:350
  72.4 1.3 fusion.23
  73.7 3.6 %multiply_add_fusion = f32[16,8,32,128]{3,1,0,2:T(8,128)S(1)} fusion(f32[16,8,32]{1,0,2:T(8,128)S(1)} %copy-done.9, f32[16,32,128]{2,0,1:T(8,128)S(1)} %bitcast.124, f32[16,32]{0,1:T(8,128)S(1)} %copy.388, f32[16,8,32]{1,0,2:T(8,128)S(1)} %copy-done.5, f32[16,32,128]{2,0,1:T(8,128)S(1)} %bitcast.121, f32[16,32]{0,1:T(8,128)S(1)} %copy.383, ...), kind=kLoop, calls=%fused_computation.14 | loop fusion | flops 4718592 | bytes 5036032 | tf_op jit(solution)/shard_map/add | solution.py:350
  77.6 1.3 fusion.24
  80.2 2.0 copy_bitcast_fusion
  82.2 14.9 %all-to-all-done = bf16[16,2,32,1024]{3,2,1,0:T(8,128)(2,1)} async-done(((bf16[16,2,32,1024]{3,2,1,0:T(8,128)(2,1)}), bf16[16,2,32,1024]{3,2,1,0:T(8,128)(2,1)}, u32[]{:S(2)}, u32[]{:S(2)}) %all-to-all-start) | async-done | bytes 2097184 | tf_op jit(solution)/shard_map/all_to_all | solution.py:279
  97.1 2.7 %fusion.32 = (bf16[1024,512]{1,0:T(8,128)(2,1)S(1)}, bf16[1024,512]{1,0:T(8,128)(2,1)}) fusion(bf16[1024,1024]{1,0:T(8,128)(2,1)} %bitcast.4), kind=kLoop, calls=%fused_computation.86 | loop fusion | bytes 4194304 | tf_op jit(solution)/shard_map/slice | solution.py:42
  99.8 2.3 %copy.344 = bf16[1024,512]{0,1:T(8,128)(2,1)} copy(bf16[1024,512]{1,0:T(8,128)(2,1)} %get-tuple-element.22) | data formatting | bytes 2097152 | tf_op jit(solution)/shard_map/slice | solution.py:45
  102.1 1.3 copy.345
  103.4 3.1 %bitcast_reduce_fusion = (f32[16,4,2,4]{0,3,1,2:T(4,128)S(1)}, f32[2,1024,16,4,4]{1,2,4,3,0:T(8,128)}) fusion(f32[2,1024]{1,0:T(2,128)S(1)} %bitcast.146, bf16[1024,2,256,1,1]{0,2,4,3,1:T(8,128)(2,1)} %bitcast.126, bf16[16,4,2,4,256]{4,3,2,1,0:T(4,128)(2,1)S(1)} %copy-done.20, pred[1024]{0:T(1024)(128)(4,1)S(1)} %copy-done.34), kind=kOutput, calls=%fused_computation.10 | convolution fusion | flops 270532096 | bytes 3419136 | tf_op jit(solution)/shard_map/btgqd,lgd->btgql/dot_general | solution.py:58
  106.7 2.7 %fusion.4 = f32[16,4,2,4]{0,3,1,2:T(4,128)} fusion(f32[2,1024,16,4,4]{1,2,4,3,0:T(8,128)} %get-tuple-element.48, f32[16,4,2,4]{0,3,1,2:T(4,128)S(1)} %max.9), kind=kLoop, calls=%fused_computation.19 | loop fusion | flops 1048064 | bytes 2101248 | tf_op jit(solution)/shard_map/reduce_sum | solution.py:78
  111.9 1.4 fusion.26
  115.9 1.3 multiply_convert_fusion.3
  117.5 5.1 %multiply_reduce_fusion.2 = (f32[64]{0:T(128)S(1)}, bf16[64,2048]{1,0:T(8,128)(2,1)S(1)}) fusion(f32[64,2048]{1,0:T(8,128)S(1)} %copy-done.4, bf16[64,2048]{1,0:T(8,128)(2,1)S(1)} %reshape.196, bf16[2048,2048]{1,0:T(8,128)(2,1)} %param.32), kind=kOutput, calls=%fused_computation.36 | convolution fusion | flops 537526208 | bytes 9437440 | tf_op jit(solution)/shard_map/dot_general | solution.py:293
  124.3 1.6 copy-done.1
  125.8 82.1 %shard_map.229 = bf16[64,2048]{1,0:T(8,128)(2,1)S(1)} custom-call(bf16[64,2176]{1,0:T(8,128)(2,1)S(1)} %concatenate.14.x_ref, bf16[2048,512]{1,0:T(8,128)(2,1)S(1)} %bitcast.109, bf16[2048,512]{1,0:T(8,128)(2,1)} %bitcast.122, bf16[512,2048]{1,0:T(8,128)(2,1)} %bitcast.123), custom_call_target="tpu_custom_call" | custom-call | tf_op jit(solution)/shard_map/pallas_call | solution.py:211
  (161 shorter events, 37.9 us)
Async XLA Ops:
  0.6 18.6 %copy-start = (bf16[32,32,1024]{2,1,0:T(8,128)(2,1)S(1)}, bf16[32,32,1024]{2,1,0:T(8,128)(2,1)}, u32[]{:S(2)}) copy-start(bf16[32,32,1024]{2,1,0:T(8,128)(2,1)} %param.22) | copy-start | bytes 6291460
  8.1 10.2 %copy-start.16 = (bf16[16,4,2048]{2,1,0:T(4,128)(2,1)S(1)}, bf16[16,4,2048]{2,1,0:T(4,128)(2,1)}, u32[]{:S(2)}) copy-start(bf16[16,4,2048]{2,1,0:T(4,128)(2,1)} %param.33) | copy-start | bytes 786436
  9.2 40.7 %all-to-all-start.1 = ((bf16[16,272,128]{2,1,0:T(8,128)(2,1)}), bf16[16,272,128]{2,1,0:T(8,128)(2,1)}, u32[]{:S(2)}, u32[]{:S(2)}) async-start(bf16[16,272,128]{2,1,0:T(8,128)(2,1)} %fusion.11), calls=%async_computation.1 | async-start | bytes 2228224 | tf_op jit(solution)/shard_map/all_to_all | solution.py:271
  19.2 2.0 copy-start.18
  19.2 2.2 %copy-start.22 = (bf16[16,4,1024]{2,1,0:T(4,128)(2,1)S(1)}, bf16[16,4,1024]{2,1,0:T(4,128)(2,1)}, u32[]{:S(2)}) copy-start(bf16[16,4,1024]{2,1,0:T(4,128)(2,1)} %param.31) | copy-start | bytes 393220
  21.2 3.0 %copy-start.33 = (bf16[2048]{0:T(1024)(128)(2,1)S(1)}, bf16[2048]{0:T(1024)(128)(2,1)}, u32[]{:S(2)}) copy-start(bf16[2048]{0:T(1024)(128)(2,1)} %param.34) | copy-start | bytes 12292
  21.2 3.6 %copy-start.30 = (s32[16,4,8]{0,2,1:T(8,128)S(1)}, s32[16,4,8]{0,2,1:T(8,128)}, u32[]{:S(2)}) copy-start(s32[16,4,8]{0,2,1:T(8,128)} %param.36) | copy-start | bytes 6148
  21.2 3.8 %copy-start.8 = (bf16[16,4,4096]{2,1,0:T(4,128)(2,1)S(1)}, bf16[16,4,4096]{2,1,0:T(4,128)(2,1)}, u32[]{:S(2)}) copy-start(bf16[16,4,4096]{2,1,0:T(4,128)(2,1)} %param.40) | copy-start | bytes 1572868
  21.4 3.5 %copy-start.19 = (bf16[16,4,2,4,256]{4,3,2,1,0:T(4,128)(2,1)}, bf16[16,4,2,4,256]{4,3,2,1,0:T(4,128)(2,1)S(1)}, u32[]{:S(2)}) copy-start(bf16[16,4,2,4,256]{4,3,2,1,0:T(4,128)(2,1)S(1)} %reshape.188) | copy-start | bytes 786436
  31.3 5.2 %copy-start.2 = (f32[16,4,16,2,128]{4,1,0,3,2:T(4,128)}, f32[16,4,16,2,128]{4,1,0,3,2:T(4,128)S(1)}, u32[]{:S(2)}) copy-start(f32[16,4,16,2,128]{4,1,0,3,2:T(4,128)S(1)} %broadcast_in_dim.76) | copy-start | bytes 3145732
  36.4 4.4 %copy-start.28 = (f32[16,4,32]{2,1,0:T(4,128)S(1)}, f32[16,4,32]{2,1,0:T(4,128)}, u32[]{:S(2)}) copy-start(f32[16,4,32]{2,1,0:T(4,128)} %param.42) | copy-start | bytes 24580
  36.4 4.5 %copy-start.29 = (f32[16,4,32]{2,1,0:T(4,128)S(1)}, f32[16,4,32]{2,1,0:T(4,128)}, u32[]{:S(2)}) copy-start(f32[16,4,32]{2,1,0:T(4,128)} %param.43) | copy-start | bytes 24580
  49.9 47.2 %all-to-all-start = ((bf16[16,2,32,1024]{3,2,1,0:T(8,128)(2,1)}), bf16[16,2,32,1024]{3,2,1,0:T(8,128)(2,1)}, u32[]{:S(2)}, u32[]{:S(2)}) async-start(bf16[16,2,32,1024]{3,2,1,0:T(8,128)(2,1)} %bitcast.114), calls=%async_computation | async-start | bytes 4194304 | tf_op jit(solution)/shard_map/all_to_all | solution.py:279
  66.6 1.7 copy-start.14
  66.6 1.7 copy-start.23
  66.6 3.0 %copy-start.5 = (f32[16,8,32]{1,0,2:T(8,128)S(1)}, f32[16,8,32]{1,0,2:T(8,128)}, u32[]{:S(2)}) copy-start(f32[16,8,32]{1,0,2:T(8,128)} %copy.387) | copy-start | bytes 49156
  69.6 2.8 %copy-start.13 = (f32[16,1,32,128]{3,2,1,0:T(8,128)S(1)}, f32[16,1,32,128]{3,2,1,0:T(8,128)}, u32[]{:S(2)}) copy-start(f32[16,1,32,128]{3,2,1,0:T(8,128)} %get-tuple-element.24) | copy-start | bytes 786436
  69.7 4.1 %copy-start.9 = (f32[16,8,32]{1,0,2:T(8,128)S(1)}, f32[16,8,32]{1,0,2:T(8,128)}, u32[]{:S(2)}) copy-start(f32[16,8,32]{1,0,2:T(8,128)} %copy.392) | copy-start | bytes 49156
  73.7 3.9 %copy-start.12 = (f32[16,1,32,128]{3,2,1,0:T(8,128)S(1)}, f32[16,1,32,128]{3,2,1,0:T(8,128)}, u32[]{:S(2)}) copy-start(f32[16,1,32,128]{3,2,1,0:T(8,128)} %get-tuple-element.23) | copy-start | bytes 786436
  73.7 5.2 %copy-start.11 = (f32[16,1,32]{1,0,2:T(8,128)S(1)}, f32[16,1,32]{1,0,2:T(8,128)}, u32[]{:S(2)}) copy-start(f32[16,1,32]{1,0,2:T(8,128)} %copy.455) | copy-start | bytes 6148
  99.7 3.7 %copy-start.20 = (bf16[16,4,2,4,256]{4,3,2,1,0:T(4,128)(2,1)S(1)}, bf16[16,4,2,4,256]{4,3,2,1,0:T(4,128)(2,1)}, u32[]{:S(2)}) copy-start(bf16[16,4,2,4,256]{4,3,2,1,0:T(4,128)(2,1)} %copy-done.19) | copy-start | bytes 786436
  99.7 3.7 %copy-start.32 = (f32[1024,2]{0,1:T(2,128)S(1)}, f32[1024,2]{0,1:T(2,128)}, u32[]{:S(2)}) copy-start(f32[1024,2]{0,1:T(2,128)} %reshape.191) | copy-start | bytes 24580
  99.8 3.7 %copy-start.34 = (pred[1024]{0:T(1024)(128)(4,1)S(1)}, pred[1024]{0:T(1024)(128)(4,1)}, u32[]{:S(2)}) copy-start(pred[1024]{0:T(1024)(128)(4,1)} %iota_compare_fusion.3) | copy-start | bytes 3076
  106.5 2.9 %copy-start.17 = (f32[16,4,2,4,4]{3,4,1,2,0:T(4,128)S(1)}, f32[16,4,2,4,4]{3,4,1,2,0:T(4,128)}, u32[]{:S(2)}) copy-start(f32[16,4,2,4,4]{3,4,1,2,0:T(4,128)} %get-tuple-element.50) | copy-start | bytes 24580
  106.7 6.6 %copy-start.10 = (bf16[1024,512]{0,1:T(8,128)(2,1)S(1)}, bf16[1024,512]{0,1:T(8,128)(2,1)}, u32[]{:S(2)}) copy-start(bf16[1024,512]{0,1:T(8,128)(2,1)} %copy.344) | copy-start | bytes 3145732
  110.4 2.9 %copy-start.31 = (f32[1024,2]{0,1:T(2,128)S(1)}, f32[1024,2]{0,1:T(2,128)}, u32[]{:S(2)}) copy-start(f32[1024,2]{0,1:T(2,128)} %reshape.193) | copy-start | bytes 24580
  111.9 1.7 copy-start.7
  114.4 3.0 %copy-start.4 = (f32[64,2048]{1,0:T(8,128)S(1)}, f32[64,2048]{1,0:T(8,128)}, u32[]{:S(2)}) copy-start(f32[64,2048]{1,0:T(8,128)} %reshape.209) | copy-start | bytes 1572868
  117.4 6.0 %copy-start.26 = (f32[2048]{0:T(1024)S(1)}, f32[2048]{0:T(1024)}, u32[]{:S(2)}) copy-start(f32[2048]{0:T(1024)} %convert_element_type.57) | copy-start | bytes 24580
  117.4 6.1 %copy-start.25 = (bf16[2048,16]{0,1:T(8,128)(2,1)S(1)}, bf16[2048,16]{0,1:T(8,128)(2,1)}, u32[]{:S(2)}) copy-start(bf16[2048,16]{0,1:T(8,128)(2,1)} %param.35) | copy-start | bytes 196612
  117.4 6.1 %copy-start.27 = (pred[64,16]{1,0:T(32,128)(4,1)S(1)}, pred[64,16]{1,0:T(32,128)(4,1)}, u32[]{:S(2)}) copy-start(pred[64,16]{1,0:T(32,128)(4,1)} %copy.370) | copy-start | bytes 3076
  124.2 1.6 copy-start.1
  (5 other events, 7.1 us)

commit v2 on v1

v2 whole, which is shorter than its diff:
```python
import functools

import jax
import jax.numpy as jnp
from jax import lax
from jax.experimental import pallas as pl
from jax.experimental.pallas import tpu as pltpu
from jax.sharding import PartitionSpec as P

MESH = pl.DeviceIdType.MESH
MIX_COLUMNS = 128

QUERY_HEADS = 8
KEY_VALUE_HEADS = 2
HEAD_SIZE = 256
DK = 128
PAGE_POSITIONS = 32
DRAFTS = 4


norm_eps = 1e-06
masked_score = -1e30


def attend_kernel(
    experts, n, q_ref, gate_ref, fresh_ref, codes_src, scales_src, live_ref, out_w_hbm,
    residual_ref, gain_ref, router_ref, named_ref, attn_ref, packed_ref,
    gated, codes_in, scales_in, out_w_ref, send_sem, recv_sem, scale_send, scale_recv, own_sem,
):
    me = lax.axis_index("ep")
    barrier = pltpu.get_barrier_semaphore()
    peers = [lax.rem(me + k, n) for k in range(n)]
    for k in range(1, n):
        pl.semaphore_signal(barrier, inc=1, device_id={"ep": peers[k]}, device_id_type=MESH)
    pl.semaphore_wait(barrier, n - 1)
    copies = []
    for k in range(1, n):
        for src, dst, s_sem, r_sem in (
            (scales_src, scales_in, scale_send, scale_recv),
            (codes_src, codes_in, send_sem, recv_sem),
        ):
            copy = pltpu.make_async_remote_copy(
                src_ref=src.at[peers[k]], dst_ref=dst.at[me], send_sem=s_sem.at[k],
                recv_sem=r_sem.at[k], device_id={"ep": peers[k]}, device_id_type=MESH,
            )
            copy.start()
            copies.append(copy)
    local = [
        pltpu.make_async_copy(codes_src.at[me], codes_in.at[me], own_sem.at[0]),
        pltpu.make_async_copy(scales_src.at[me], scales_in.at[me], own_sem.at[1]),
        pltpu.make_async_copy(out_w_hbm, out_w_ref, own_sem.at[2]),
    ]
    for copy in local:
        copy.start()
    for copy in copies + local:
        copy.wait()
    scales = jnp.concatenate(
        [
            scales_in[2 * i].astype(jnp.float32) + scales_in[2 * i + 1].astype(jnp.float32)
            for i in range(n // 2)
        ],
        axis=1,
    )
    length = live_ref.shape[1]

    def codes(columns):
        return codes_in[:, :, columns].reshape(length, HEAD_SIZE)

    count = q_ref.shape[0]
    groups = QUERY_HEADS // KEY_VALUE_HEADS
    half = KEY_VALUE_HEADS * HEAD_SIZE
    factor = HEAD_SIZE ** (-0.5)
    across_last = (((1,), (1,)), ((), ()))
    row = lax.broadcasted_iota(jnp.int32, (groups * count, count), 0) % count
    column = lax.broadcasted_iota(jnp.int32, (groups * count, count), 1)
    causal = (row // DRAFTS == column // DRAFTS) & (column <= row)
    live = live_ref[...] > 0.0
    for g in range(KEY_VALUE_HEADS):
        q = jnp.concatenate(
            [
                q_ref[:, (g * groups + i) * HEAD_SIZE : (g * groups + i + 1) * HEAD_SIZE]
                for i in range(groups)
            ],
            axis=0,
        )
        keys = slice(g * HEAD_SIZE, (g + 1) * HEAD_SIZE)
        values = slice(half + g * HEAD_SIZE, half + (g + 1) * HEAD_SIZE)
        cached = lax.dot_general(
            q, codes(keys), across_last, preferred_element_type=jnp.float32
        )
        cached = jnp.where(live, cached * scales[g : g + 1] * factor, masked_score)
        own = lax.dot_general(
            q, fresh_ref[:, keys], across_last, preferred_element_type=jnp.float32
        )
        own = jnp.where(causal, own * factor, masked_score)
        top = jnp.maximum(
            jnp.max(cached, axis=1, keepdims=True), jnp.max(own, axis=1, keepdims=True)
        )
        cached = jnp.exp(cached - top)
        own = jnp.exp(own - top)
        scale = 1.0 / (
            jnp.sum(cached, axis=1, keepdims=True) + jnp.sum(own, axis=1, keepdims=True)
        )
        cached = (cached * scale * scales[KEY_VALUE_HEADS + g : KEY_VALUE_HEADS + g + 1]).astype(jnp.bfloat16)
        own = (own * scale).astype(jnp.bfloat16)
        mixed = jnp.dot(cached, codes(values), preferred_element_type=jnp.float32)
        mixed = mixed + jnp.dot(own, fresh_ref[:, values], preferred_element_type=jnp.float32)
        for i in range(groups):
            head = slice((g * groups + i) * HEAD_SIZE, (g * groups + i + 1) * HEAD_SIZE)
            gate = jax.nn.sigmoid(gate_ref[:, head].astype(jnp.float32))
            gated[:, head] = (mixed[i * count : (i + 1) * count] * gate).astype(jnp.bfloat16)
    attn = jnp.dot(gated[...], out_w_ref[...], preferred_element_type=jnp.float32).astype(
        jnp.bfloat16
    )
    attn_ref[...] = attn
    hidden = residual_ref[...].astype(jnp.float32) + attn.astype(jnp.float32)
    normed = (
        hidden
        * lax.rsqrt(jnp.mean(hidden * hidden, axis=1, keepdims=True) + norm_eps)
        * gain_ref[...]
    ).astype(jnp.bfloat16)
    width = normed.shape[1]
    packed_ref[:, :width] = normed
    logits = jnp.dot(normed, router_ref[...], preferred_element_type=jnp.float32)
    named = named_ref[...] > 0.0
    logits = jnp.where(named, logits, masked_score)
    raised = jnp.where(named, jnp.exp(logits - jnp.max(logits, axis=1, keepdims=True)), 0.0)
    lane = lax.broadcasted_iota(jnp.int32, raised.shape, 1)
    mixing = raised / jnp.sum(jnp.where(lane < experts, raised, 0.0), axis=1, keepdims=True)
    coarse = mixing.astype(jnp.bfloat16)
    fine = (mixing - coarse.astype(jnp.float32)).astype(jnp.bfloat16)
    packed_ref[:, width:] = jnp.where(
        lane < experts, coarse.astype(jnp.float32), fine.astype(jnp.float32)
    ).astype(jnp.bfloat16)


def attend(experts, *operands):
    count, width = operands[0].shape
    whole = pl.BlockSpec(memory_space=pltpu.VMEM)
    specs = [whole] * len(operands)
    specs[3] = specs[6] = pl.BlockSpec(memory_space=pl.ANY)
    n = operands[3].shape[0]
    dma = pltpu.SemaphoreType.DMA
    return pl.pallas_call(
        functools.partial(attend_kernel, experts, n),
        out_shape=(
            jax.ShapeDtypeStruct((count, width), jnp.bfloat16),
            jax.ShapeDtypeStruct((count, width + MIX_COLUMNS), jnp.bfloat16),
        ),
        in_specs=specs,
        out_specs=(whole, whole),
        scratch_shapes=[
            pltpu.VMEM((count, width), jnp.bfloat16),
            pltpu.VMEM(operands[3].shape, jnp.bfloat16),
            pltpu.VMEM(operands[4].shape, jnp.bfloat16),
            pltpu.VMEM(operands[6].shape, jnp.bfloat16),
            dma((n,)), dma((n,)), dma((n,)), dma((n,)), dma((3,)),
        ],
        compiler_params=pltpu.CompilerParams(
            collective_id=0, has_side_effects=True, vmem_limit_bytes=50 * 1024 * 1024
        ),
    )(*operands)


def delta_heads(qk_ref, v_ref, decay_ref, beta_ref, state_ref, out_ref, first, last):
    beams = qk_ref.shape[0] // DRAFTS
    half = qk_ref.shape[1] // 2
    local = state_ref.shape[1]
    heads = state_ref.shape[0] * local
    pairs = heads // (half // DK)
    lane = lax.broadcasted_iota(jnp.int32, decay_ref.shape, 1)

    def rows(x, t):
        return x[t * beams : (t + 1) * beams]

    def product(x, y):
        return jnp.sum(x * y, axis=1, keepdims=True)

    def one(j, carry):
        start = pl.multiple_of(j * DK, DK)
        key_start = pl.multiple_of(half + j * DK, DK)
        q = qk_ref[:, pl.ds(start, DK)].astype(jnp.float32)
        k = qk_ref[:, pl.ds(key_start, DK)].astype(jnp.float32)
        q = q * lax.rsqrt(product(q, q) + norm_eps) * DK ** (-0.5)
        k = k * lax.rsqrt(product(k, k) + norm_eps)
        probes = jnp.concatenate([k, q], axis=0)
        coarse = probes.astype(jnp.bfloat16)
        fine = (probes - coarse.astype(jnp.float32)).astype(jnp.bfloat16)
        probes = jnp.concatenate([coarse, fine], axis=0)
        half_rows = 2 * DRAFTS * beams
        along_key = {
            (s, t): product(rows(k, s), rows(k, t)) for t in range(DRAFTS) for s in range(t)
        }
        along_query = {
            (s, t): product(rows(k, s), rows(q, t)) for t in range(DRAFTS) for s in range(t + 1)
        }
        for part in range(pairs):
            head = j * pairs + part
            images = jnp.dot(
                probes, state_ref[head // local, head % local], preferred_element_type=jnp.float32)
            images = images[:half_rows] + images[half_rows:]
            decay = jnp.sum(jnp.where(lane == head, decay_ref[...], 0.0), axis=1, keepdims=True)
            beta = jnp.sum(jnp.where(lane == head, beta_ref[...], 0.0), axis=1, keepdims=True)
            columns = pl.ds(pl.multiple_of(head * DK, DK), DK)
            v = v_ref[:, columns].astype(jnp.float32)
            kept = None
            weights, writes = [], []
            for t in range(DRAFTS):
                seen = rows(images, t) if kept is None else kept * rows(images, t)
                for s in range(t):
                    seen = seen + (weights[s] * along_key[s, t]) * writes[s]
                now = rows(decay, t)
                writes.append(rows(v, t) - now * seen)
                kept = now if kept is None else kept * now
                weights = [now * w for w in weights] + [rows(beta, t)]
                got = kept * rows(images, DRAFTS + t)
                for s in range(t + 1):
                    got = got + (weights[s] * along_query[s, t]) * writes[s]
                out_ref[t * beams : (t + 1) * beams, columns] = got.astype(jnp.bfloat16)
        return carry

    lax.fori_loop(first, last, one, 0)


def expert_kernel(
    n, x_ref, gate_hbm, up_hbm, down_hbm, qk_hbm, v_hbm, decay_ref, beta_ref, state_src,
    out_ref, delta_ref, rows_in, part, core_in, y_in, z_in,
    z_send, z_recv, y_send, y_recv, c_send, c_recv,
    core_send, core_recv, fold_send, fold_recv, last_send, last_recv, own_sem,
    gate_ref, up_ref, down_ref, qk_ref, v_ref, state_ref, state_send, state_recv,
):
    deep = n // 4
    width = out_ref.shape[1]
    count = out_ref.shape[0]
    me = lax.axis_index("ep")
    c = lax.rem(me, 2)
    y = lax.rem(me // 2, 2)
    z = me // 4

    def at(zz, yy, cc):
        return (zz * 2 + yy) * 2 + cc

    other = at(z, y, 1 - c)
    across = at(z, 1 - y, c)
    near = jnp.minimum(z, deep - 1 - z)
    turn = [z]
    for k in range(1, deep):
        close = z - (k + 1) // 2 if k % 2 else z + k // 2
        far = jnp.where(z > near, z - (k - near), z + (k - near))
        turn.append(jnp.where(k <= 2 * near, close, far))
    peers = [lax.rem(me + k, n) for k in range(1, n)]
    barrier = pltpu.get_barrier_semaphore()
    for peer in peers:
        pl.semaphore_signal(barrier, inc=1, device_id={"ep": peer}, device_id_type=MESH)
    pl.semaphore_wait(barrier, len(peers))

    def send(src, dst, s_sem, r_sem, peer):
        copy = pltpu.make_async_remote_copy(
            src_ref=src, dst_ref=dst, send_sem=s_sem, recv_sem=r_sem,
            device_id={"ep": peer}, device_id_type=MESH,
        )
        copy.start()
        return copy

    local = [
        pltpu.make_async_copy(src, dst, own_sem.at[i])
        for i, (src, dst) in enumerate((
            (x_ref, rows_in.at[me]), (gate_hbm, gate_ref), (up_hbm, up_ref),
            (down_hbm, down_ref), (qk_hbm, qk_ref), (v_hbm, v_ref),
            (state_src.at[me], state_ref.at[me]),
        ))
    ]
    y_copies = {0: send(x_ref, rows_in.at[me], y_send.at[0], y_recv.at[0], across)}

    def pass_on(src, block, origin, k, target):
        return pltpu.make_async_remote_copy(
            src_ref=src, dst_ref=rows_in.at[block], send_sem=z_send.at[k],
            recv_sem=z_recv.at[origin], device_id={"ep": at(target, y, c)}, device_id_type=MESH,
        )

    above, below = lax.rem(z + 1, deep), lax.rem(z + deep - 1, deep)

    @pl.when(z + 1 < deep)
    def _():
        pass_on(x_ref, me, z, 0, above).start()

    @pl.when(z > 0)
    def _():
        pass_on(x_ref, me, z, deep, below).start()

    c_copies = {(0, 0): send(x_ref, rows_in.at[me], c_send.at[0], c_recv.at[0], other)}
    for copy in local:
        copy.start()
    state_copies = {
        k: send(
            state_src.at[peers[k - 1]], state_ref.at[me], state_send.at[k], state_recv.at[k],
            peers[k - 1],
        )
        for k in range(1, n)
    }
    core_copies, fold_copies, last_copies = {}, {}, {}
    lanes = lax.broadcasted_iota(jnp.int32, (4 * count, MIX_COLUMNS), 1)
    picked = (lanes == me) | (lanes == me + n)

    def onward(k):
        block = at(turn[k], y, c)
        target = jnp.where(turn[k] < z, above, below)
        goes = jnp.where(turn[k] < z, z + 1 < deep, z > 0)
        return goes, pass_on(rows_in.at[block], block, turn[k], k, target)

    def stage(k):
        block = at(turn[k], y, c)
        goes, copy = onward(k)
        copy.wait_recv()

        @pl.when(goes)
        def _():
            copy.start()

        y_copies[k] = send(rows_in.at[block], rows_in.at[block], y_send.at[k], y_recv.at[k], across)
        c_copies[k, 0] = send(
            rows_in.at[block], rows_in.at[block], c_send.at[2 * k], c_recv.at[2 * k], other
        )

    key_heads = qk_ref.shape[1] // (2 * DK)

    def delta(first, last):
        delta_heads(
            qk_ref, v_ref, decay_ref, beta_ref, state_ref, delta_ref, first, last
        )

    def fold_y(k):
        y_here = at(turn[k], y, c)
        fold_copies[k].wait_recv()
        part[y_here] = (
            part[y_here].astype(jnp.float32) + y_in[k].astype(jnp.float32)
        ).astype(jnp.bfloat16)
        if k:
            last_copies[k] = send(
                part.at[y_here], z_in.at[z], last_send.at[k], last_recv.at[z], y_here
            )

    for k in range(deep):
        y_copies[k].wait_recv()
        block = at(turn[k], 1 - y, c)
        c_copies[k, 1] = send(
            rows_in.at[block], rows_in.at[block], c_send.at[2 * k + 1], c_recv.at[2 * k + 1], other
        )
        if k + 1 < deep:
            stage(k + 1)
        if k == 0:
            for copy in local:
                copy.wait()
        c_copies[k, 0].wait_recv()
        c_copies[k, 1].wait_recv()
        first = pl.multiple_of(turn[k] * 4, 4)
        rows = rows_in[pl.ds(first, 4)].reshape(4 * count, -1)
        mix = jnp.sum(
            jnp.where(picked, rows[:, width:].astype(jnp.float32), 0.0), axis=1, keepdims=True
        )
        rows = rows[:, :width]
        gate_val = jnp.dot(rows, gate_ref[...], preferred_element_type=jnp.float32)
        up_val = jnp.dot(rows, up_ref[...], preferred_element_type=jnp.float32)
        inner = (gate_val * jax.nn.sigmoid(gate_val) * up_val).astype(jnp.bfloat16)
        made = jnp.dot(inner, down_ref[...], preferred_element_type=jnp.float32)
        part[pl.ds(first, 4)] = (made * mix).astype(jnp.bfloat16).reshape(4, count, width)
        for yy in range(2):
            core_copies[k, yy] = send(
                part.at[at(turn[k], yy, 1 - c)], core_in.at[2 * k + yy],
                core_send.at[2 * k + yy], core_recv.at[2 * k + yy], other,
            )
        for yy in range(2):
            core_copies[k, yy].wait_recv()
            here = at(turn[k], yy, c)
            part[here] = (
                part[here].astype(jnp.float32) + core_in[2 * k + yy].astype(jnp.float32)
            ).astype(jnp.bfloat16)
        fold_copies[k] = send(
            part.at[at(turn[k], 1 - y, c)], y_in.at[k], fold_send.at[k], fold_recv.at[k], across
        )
        if k:
            fold_y(k - 1)
    for copy in state_copies.values():
        copy.wait_recv()
    delta(0, key_heads // 2)
    fold_y(deep - 1)
    delta(key_heads // 2, key_heads)
    total = part[me].astype(jnp.float32)
    for k in range(1, deep):
        pltpu.make_async_remote_copy(
            src_ref=part.at[me], dst_ref=z_in.at[turn[k]], send_sem=last_send.at[k],
            recv_sem=last_recv.at[turn[k]], device_id={"ep": other}, device_id_type=MESH,
        ).wait_recv()
        total = total + z_in[turn[k]].astype(jnp.float32)
    out_ref[...] = total.astype(jnp.bfloat16)
    @pl.when(z + 1 < deep)
    def _():
        pass_on(x_ref, me, z, 0, above).wait_send()

    @pl.when(z > 0)
    def _():
        pass_on(x_ref, me, z, deep, below).wait_send()

    for k in range(1, deep):
        goes, copy = onward(k)

        @pl.when(goes)
        def _():
            copy.wait_send()

    for group in (state_copies, y_copies, c_copies, core_copies, fold_copies, last_copies):
        for copy in group.values():
            copy.wait_send()


def routed_experts(packed, gate_w, up_w, down_w, qk, v, decay, beta, states, n):
    count = packed.shape[0]
    width = down_w.shape[1]
    deep = n // 4
    dma = pltpu.SemaphoreType.DMA
    return pl.pallas_call(
        functools.partial(expert_kernel, n),
        out_shape=(
            jax.ShapeDtypeStruct((count, width), jnp.bfloat16),
            jax.ShapeDtypeStruct(v.shape, jnp.bfloat16),
        ),
        in_specs=[
            pl.BlockSpec(memory_space=pl.ANY if i in (1, 2, 3, 4, 5, 8) else pltpu.VMEM)
            for i in range(9)
        ],
        out_specs=(pl.BlockSpec(memory_space=pltpu.VMEM), pl.BlockSpec(memory_space=pltpu.VMEM)),
        scratch_shapes=[
            pltpu.VMEM((n, count, packed.shape[1]), jnp.bfloat16),
            pltpu.VMEM((n, count, width), jnp.bfloat16),
            pltpu.VMEM((2 * deep, count, width), jnp.bfloat16),
            pltpu.VMEM((deep, count, width), jnp.bfloat16),
            pltpu.VMEM((deep, count, width), jnp.bfloat16),
            dma((deep + 1,)), dma((deep,)), dma((deep,)), dma((deep,)),
            dma((2 * deep,)), dma((2 * deep,)), dma((2 * deep,)), dma((2 * deep,)),
            dma((deep,)), dma((deep,)), dma((deep,)), dma((deep,)), dma((7,)),
            *(pltpu.VMEM(x.shape, jnp.bfloat16) for x in (gate_w, up_w, down_w, qk, v, states)),
            dma((n,)), dma((n,)),
        ],
        compiler_params=pltpu.CompilerParams(
            collective_id=1, has_side_effects=True, vmem_limit_bytes=50 * 1024 * 1024
        ),
    )(packed, gate_w, up_w, down_w, qk, v, decay, beta, states)


def on_device(
    page_key_value_codes,
    page_key_scales,
    page_value_scales,
    block_table,
    prompt_lengths,
    decode_owner,
    prefill_states,
    att_query,
    att_gate,
    draft_keys_values,
    out_weight,
    residual,
    norm_gain,
    router_weight,
    expert_routes,
    gate_weight,
    up_weight,
    down_weight,
    gdn_qk,
    gdn_v,
    gdn_decay,
    gdn_beta,
):
    devices = lax.axis_size("ep")
    device_id = lax.axis_index("ep")
    labels = jnp.arange(devices, dtype=jnp.int32)
    matches = (decode_owner[:, None] == labels[None, :]).astype(jnp.int32)
    inverse = jnp.sum(labels[:, None] * matches, axis=0)
    page_ids = block_table[inverse]
    scales = jnp.concatenate([page_key_scales[page_ids], page_value_scales[page_ids]], axis=-1)
    scales = jnp.repeat(scales, PAGE_POSITIONS, axis=1).transpose(0, 2, 1)
    scales = jnp.pad(scales, ((0, 0), (0, 16 - scales.shape[1]), (0, 0)))
    blank = jnp.zeros_like(scales)
    scales = jnp.where(
        device_id % 2 == 0,
        jnp.concatenate([scales, blank], axis=2),
        jnp.concatenate([blank, scales], axis=2),
    )
    codes = page_key_value_codes[page_ids]
    codes = codes.reshape(devices, -1, codes.shape[-1])
    states = prefill_states[inverse]
    length = prompt_lengths[inverse[device_id]]
    live = (jnp.arange(devices * codes.shape[1], dtype=jnp.int32) < length).astype(jnp.float32)[None]
    beam_total, draft_tokens, width = att_query.shape
    row_count = beam_total * draft_tokens

    def flat(x):
        return x.reshape(row_count, -1)

    def by_draft(x):
        return x.transpose(1, 0, 2).reshape(row_count, -1)

    experts = router_weight.shape[1]
    spare = MIX_COLUMNS - 2 * experts
    router = jnp.concatenate([router_weight, router_weight], axis=1)
    router = jnp.pad(router, ((0, 0), (0, spare)))
    named = jnp.any(
        flat(expert_routes)[:, :, None] == jnp.arange(experts, dtype=jnp.int32)[None, None, :],
        axis=1,
    ).astype(jnp.float32)
    named = jnp.pad(jnp.concatenate([named, named], axis=1), ((0, 0), (0, spare)))
    attn_mix, packed = attend(
        experts,
        flat(att_query),
        flat(att_gate),
        flat(draft_keys_values),
        codes,
        scales,
        live,
        out_weight,
        flat(residual),
        norm_gain.astype(jnp.float32)[None],
        router,
        named,
    )
    moe_out, gdn_out = routed_experts(
        packed, gate_weight[0], up_weight[0], down_weight[0],
        by_draft(gdn_qk), by_draft(gdn_v), by_draft(gdn_decay), by_draft(gdn_beta), states, devices,
    )
    return (
        attn_mix.reshape(att_query.shape),
        moe_out.reshape(att_query.shape),
        gdn_out.reshape(draft_tokens, beam_total, -1).transpose(1, 0, 2),
    )


def solution(mesh):
    placed = (
        P(("grp", "ep"), None, None),
        P(("grp", "ep"), None),
        P(("grp", "ep"), None),
        P("grp", "ep"),
        P("grp"),
        P("grp"),
        P("grp", "ep", None, None),
        P(("grp", "ep"), None, None),
        P(("grp", "ep"), None, None),
        P(("grp", "ep"), None, None),
        P(),
        P(("grp", "ep"), None, None),
        P(),
        P(),
        P(("grp", "ep"), None, None),
        P("ep", None, None),
        P("ep", None, None),
        P("ep", None, None),
        P(("grp", "ep"), None, None),
        P(("grp", "ep"), None, None),
        P(("grp", "ep"), None, None),
        P(("grp", "ep"), None, None),
    )
    return jax.shard_map(
        on_device,
        mesh=mesh,
        in_specs=placed,
        out_specs=(
            P(("grp", "ep"), None, None),
            P(("grp", "ep"), None, None),
            P(("grp", "ep"), None, None),
        ),
        check_vma=False,
    )
```

time: 210 us -> 169 us (0.80)
  Pallas kernels: 82.1 us -> 136 us
  local copies, waits for them, and re-layouts: 51.4 us -> 26.4 us
  other arithmetic: 26 us -> 3.12 us
  matrix products: 17.9 us -> 0 us
  waiting for transfers between devices: 14.9 us -> 0 us
  starting transfers between devices: 13.5 us -> 0 us
    pallas_call x1 -> x2, Pallas kernels: 82.1 us -> 136 us  [the longest x1 90.8 us: routed_experts(): pl.pallas_call(functools.partial(expert_kernel, n), out_shape=(jax.ShapeD...]
    dot_general x8 -> x0, matrix products: 17.9 us -> none  [the longest x1 5.1 us: on_device(): jnp.dot(gated_out.reshape(row_count, -1), out_weight, preferred_element_t...]
    slice x16 -> x0, local copies, waits for them, and re-layouts: 16.2 us -> none  [the longest x2 3.98 us: attend_prompt(): codes_by_row[:, :KEY_VALUE_HEADS * HEAD_SIZE]]
    all_to_all x2 -> x0, waiting for transfers between devices: 14.9 us -> none  [the longest x1 14.9 us: on_device(): lax.all_to_all(page_key_value_codes[page_ids], 'ep', split_axis=0, concat...]
    all_to_all x2 -> x0, starting transfers between devices: 13.5 us -> none  [the longest x1 7.43 us: on_device(): lax.all_to_all(jnp.concatenate([states, scales], axis=1), 'ep', split_axi...]
    add x4 -> x0, other arithmetic: 8.25 us -> none  [the longest x3 7.5 us: on_device(): decay_now * cache_images]
    mul x6 -> x0, other arithmetic: 5.56 us -> none  [the longest x4 5.16 us: on_device(): write_rate * (value_vec[:, draft_idx][:, None] - decay_now * keyed_image)]
    mul x13 -> x0, local copies, waits for them, and re-layouts: 4.94 us -> none  [the longest x7 3.44 us: on_device(): write_rate * (value_vec[:, draft_idx][:, None] - decay_now * keyed_image)]
  transfers between devices with their start and end apart: 2 -> 0, of which waited for: 1 -> 0; matrix products, arithmetic and copies ran while one was open for 27% -> 0% of each run, Pallas kernels for 0% -> 0%
where the time goes in v2:
time: 169 us
  Pallas kernels  136 us (80%)
  local copies, waits for them, and re-layouts  26.4 us (16%)
  other arithmetic  3.12 us (2%)
  between operations  2.83 us (2%)
    pallas_call x1, Pallas kernels, routed_experts(): pl.pallas_call(functools.partial(expert_kernel, n), out_shape=(jax.ShapeD...  90.8 us
    pallas_call x1, Pallas kernels, attend(): pl.pallas_call(functools.partial(attend_kernel, experts, n), out_shape=(j...  45.6 us
    unnamed x26, local copies, waits for them, and re-layouts  5.95 us

profile of v2, /device:TPU:0, one launch (start us, length us, event | category | flops | bytes accessed | tf_op | source)
XLA Modules:
  0.0 168.8 jit_solution(14236527052710130371)
XLA Ops:
  0.7 0.9 select_reduce_fusion
  1.6 0.8 copy.73
  2.3 0.6 gather_fusion
  3.2 0.8 copy.76
  3.9 0.6 gather_fusion.2
  4.5 0.2 copy.91
  4.7 0.8 copy.78
  5.5 0.6 gather_fusion.3
  6.1 0.2 copy.92
  6.6 0.7 pad_select_fusion.scales_src
  7.3 0.6 dynamic_slice.6
  9.8 1.2 dynamic_slice.7
  11.1 0.7 compare_convert_fusion.live_ref
  11.8 2.0 %gather_fusion.1 = bf16[32,32,1024]{2,1,0:T(8,128)(2,1)} fusion(bf16[32,32,1024]{2,1,0:T(8,128)(2,1)S(1)} %copy-done, s32[1024]{0:T(1024)S(1)} %pad_clamp_fusion), kind=kCustom, calls=%fused_computation.1 | custom fusion | bytes 4194432 | tf_op jit(solution)/shard_map/gather | solution.py:489
  13.8 0.3 copy.81
  14.3 1.0 reshape.84.gate_ref
  15.3 1.0 reshape.88.residual_ref
  16.3 0.9 reshape.85.fresh_ref
  17.3 1.4 copy.82
  18.7 0.8 copy.83
  19.7 0.7 broadcast_in_dim.9
  20.4 0.8 copy-done.3
  21.3 45.6 %shard_map.229 = (bf16[64,2048]{1,0:T(8,128)(2,1)S(1)}, bf16[64,2176]{1,0:T(8,128)(2,1)S(1)}) custom-call(bf16[64,2048]{1,0:T(8,128)(2,1)S(1)} %reshape.83.q_ref, bf16[64,2048]{1,0:T(8,128)(2,1)S(1)} %reshape.84.gate_ref, bf16[64,1024]{1,0:T(8,128)(2,1)S(1)} %reshape.85.fresh_ref, bf16[16,64,1024]{2,1,0:T(8,128)(2,1)} %bitcast.39, ...), custom_call_target="tpu_custom_call" | custom-call | tf_op jit(solution)/shard_map/pallas_call | solution.py:144
  66.9 0.7 copy-done.1
  67.6 0.7 copy-done.4
  68.3 2.1 %gather_fusion.4 = bf16[16,2,128,128]{3,2,1,0:T(8,128)(2,1)S(1)} fusion(bf16[16,2,128,128]{3,2,1,0:T(8,128)(2,1)} %param.28, s32[1024]{0:T(1024)} %copy-done.10), kind=kCustom, calls=%fused_computation.4 | custom fusion | bytes 2097216 | tf_op jit(solution)/shard_map/gather | solution.py:491
  70.5 1.3 copy.86
  71.8 1.3 copy.87
  73.2 90.8 %shard_map.230 = (bf16[64,2048]{1,0:T(8,128)(2,1)S(1)}, bf16[64,4096]{1,0:T(8,128)(2,1)S(1)}) custom-call(bf16[64,2176]{1,0:T(8,128)(2,1)S(1)} %copy-done.2, bf16[2048,512]{1,0:T(8,128)(2,1)} %bitcast.40, bf16[2048,512]{1,0:T(8,128)(2,1)} %bitcast.41, bf16[512,2048]{1,0:T(8,128)(2,1)} %bitcast.42, bf16[64,4096]{1,0:T(8,128)(2,1)S(1)} %bitcast.33, ...), custom_call_target="tpu_custom_call" | custom-call | tf_op jit(solution)/shard_map/pallas_call | solution.py:421
  164.1 1.2 copy.94
  165.3 1.8 %reshape.94 = bf16[16,4,2048]{2,1,0:T(4,128)(2,1)} reshape(bf16[64,2048]{1,0:T(8,128)(2,1)} %copy-done.5) | data formatting | bytes 524288 | tf_op jit(solution)/shard_map/reshape | solution.py:532
  167.0 1.8 %reshape.89 = bf16[16,4,2048]{2,1,0:T(4,128)(2,1)} reshape(bf16[64,2048]{1,0:T(8,128)(2,1)} %copy-done.4) | data formatting | bytes 524288 | tf_op jit(solution)/shard_map/reshape | solution.py:531
  (40 shorter events, 1.0 us)
Async XLA Ops:
  0.6 11.1 %copy-start = (bf16[32,32,1024]{2,1,0:T(8,128)(2,1)S(1)}, bf16[32,32,1024]{2,1,0:T(8,128)(2,1)}, u32[]{:S(2)}) copy-start(bf16[32,32,1024]{2,1,0:T(8,128)(2,1)} %param.22) | copy-start | bytes 6291460
  1.6 1.6 copy-start.10
  11.7 2.1 %copy-start.7 = (bf16[2048,16]{0,1:T(8,128)(2,1)S(1)}, bf16[2048,16]{0,1:T(8,128)(2,1)}, u32[]{:S(2)}) copy-start(bf16[2048,16]{0,1:T(8,128)(2,1)} %param.35) | copy-start | bytes 196612
  11.8 2.5 %copy-start.6 = (bf16[16,4,2048]{2,1,0:T(4,128)(2,1)S(1)}, bf16[16,4,2048]{2,1,0:T(4,128)(2,1)}, u32[]{:S(2)}) copy-start(bf16[16,4,2048]{2,1,0:T(4,128)(2,1)} %param.29) | copy-start | bytes 786436
  20.4 0.8 copy-start.3
  66.9 0.7 copy-start.1
  67.6 0.7 copy-start.4
  68.3 4.8 %copy-start.8 = (f32[16,4,32]{2,1,0:T(4,128)S(1)}, f32[16,4,32]{2,1,0:T(4,128)}, u32[]{:S(2)}) copy-start(f32[16,4,32]{2,1,0:T(4,128)} %param.42) | copy-start | bytes 24580
  68.3 4.9 %copy-start.9 = (f32[16,4,32]{2,1,0:T(4,128)S(1)}, f32[16,4,32]{2,1,0:T(4,128)}, u32[]{:S(2)}) copy-start(f32[16,4,32]{2,1,0:T(4,128)} %param.43) | copy-start | bytes 24580
  68.3 4.9 %copy-start.2 = (bf16[64,2176]{1,0:T(8,128)(2,1)S(1)}, bf16[64,2176]{1,0:T(8,128)(2,1)}, u32[]{:S(2)}) copy-start(bf16[64,2176]{1,0:T(8,128)(2,1)} %copy-done.1) | copy-start | bytes 835588
  164.1 1.2 copy-start.5

commit v3 on v2

--- a/solution.py
+++ b/solution.py
@@ -477,7 +477,7 @@
     matches = (decode_owner[:, None] == labels[None, :]).astype(jnp.int32)
     inverse = jnp.sum(labels[:, None] * matches, axis=0)
     page_ids = block_table[inverse]
-    scales = jnp.concatenate([page_key_scales[page_ids], page_value_scales[page_ids]], axis=-1)
+    scales = jnp.concatenate([page_key_scales, page_value_scales], axis=1)[page_ids]
     scales = jnp.repeat(scales, PAGE_POSITIONS, axis=1).transpose(0, 2, 1)
     scales = jnp.pad(scales, ((0, 0), (0, 16 - scales.shape[1]), (0, 0)))
     blank = jnp.zeros_like(scales)

time: 169 us -> 168 us (level)
  local copies, waits for them, and re-layouts: 26.4 us -> 24.1 us
    unnamed x26 -> x24, local copies, waits for them, and re-layouts: 5.95 us -> 4.45 us
where the time goes in v3:
time: 168 us; the launch traced here: 167 us
  Pallas kernels  136 us (81%)
  local copies, waits for them, and re-layouts  24.1 us (14%)
  other arithmetic  3.79 us (2%)
  between operations  2.82 us (2%)
    pallas_call x1, Pallas kernels, routed_experts(): pl.pallas_call(functools.partial(expert_kernel, n), out_shape=(jax.ShapeD...  90.8 us
    pallas_call x1, Pallas kernels, attend(): pl.pallas_call(functools.partial(attend_kernel, experts, n), out_shape=(j...  45.6 us
    unnamed x24, local copies, waits for them, and re-layouts  4.45 us

profile of v3, /device:TPU:0, one launch (start us, length us, event | category | flops | bytes accessed | tf_op | source)
XLA Modules:
  0.0 167.2 jit_solution(3665476042211362595)
XLA Ops:
  0.7 0.9 select_reduce_fusion
  1.6 0.8 copy.64
  2.3 0.6 gather_fusion
  3.2 0.7 pad_maximum_fusion.1
  3.9 0.1 copy.67
  4.0 0.6 gather_fusion.2
  4.6 0.2 copy.68
  4.8 0.1 broadcast_in_dim.6
  5.0 0.7 pad_select_fusion.scales_src
  5.8 0.6 dynamic_slice.6
  8.3 1.2 dynamic_slice.7
  9.5 0.7 compare_convert_fusion.live_ref
  10.2 2.0 %gather_fusion.1 = bf16[32,32,1024]{2,1,0:T(8,128)(2,1)} fusion(bf16[32,32,1024]{2,1,0:T(8,128)(2,1)S(1)} %copy-done, s32[1024]{0:T(1024)S(1)} %pad_clamp_fusion), kind=kCustom, calls=%fused_computation.1 | custom fusion | bytes 4194432 | tf_op jit(solution)/shard_map/gather | solution.py:489
  12.3 0.3 copy.69
  12.6 0.1 pad.17.router_ref
  12.8 1.0 reshape.84.gate_ref
  13.8 1.0 reshape.88.residual_ref
  14.8 0.9 reshape.85.fresh_ref
  15.7 1.4 copy.70
  17.1 0.8 copy.71
  18.2 0.7 broadcast_in_dim.9
  18.9 0.8 copy-done.3
  19.7 45.6 %shard_map.229 = (bf16[64,2048]{1,0:T(8,128)(2,1)S(1)}, bf16[64,2176]{1,0:T(8,128)(2,1)S(1)}) custom-call(bf16[64,2048]{1,0:T(8,128)(2,1)S(1)} %reshape.83.q_ref, bf16[64,2048]{1,0:T(8,128)(2,1)S(1)} %reshape.84.gate_ref, bf16[64,1024]{1,0:T(8,128)(2,1)S(1)} %reshape.85.fresh_ref, bf16[16,64,1024]{2,1,0:T(8,128)(2,1)} %bitcast.38, ...), custom_call_target="tpu_custom_call" | custom-call | tf_op jit(solution)/shard_map/pallas_call | solution.py:144
  65.4 0.7 copy-done.1
  66.1 0.7 copy-done.4
  66.8 2.1 %gather_fusion.3 = bf16[16,2,128,128]{3,2,1,0:T(8,128)(2,1)S(1)} fusion(bf16[16,2,128,128]{3,2,1,0:T(8,128)(2,1)} %param.28, s32[1024]{0:T(1024)} %copy-done.10), kind=kCustom, calls=%fused_computation.3 | custom fusion | bytes 2097216 | tf_op jit(solution)/shard_map/gather | solution.py:491
  68.9 1.3 copy.74
  70.3 1.3 copy.75
  71.7 90.8 %shard_map.230 = (bf16[64,2048]{1,0:T(8,128)(2,1)S(1)}, bf16[64,4096]{1,0:T(8,128)(2,1)S(1)}) custom-call(bf16[64,2176]{1,0:T(8,128)(2,1)S(1)} %copy-done.2, bf16[2048,512]{1,0:T(8,128)(2,1)} %bitcast.39, bf16[2048,512]{1,0:T(8,128)(2,1)} %bitcast.40, bf16[512,2048]{1,0:T(8,128)(2,1)} %bitcast.41, bf16[64,4096]{1,0:T(8,128)(2,1)S(1)} %bitcast.32, ...), custom_call_target="tpu_custom_call" | custom-call | tf_op jit(solution)/shard_map/pallas_call | solution.py:421
  162.5 1.2 copy.80
  163.7 1.8 %reshape.94 = bf16[16,4,2048]{2,1,0:T(4,128)(2,1)} reshape(bf16[64,2048]{1,0:T(8,128)(2,1)} %copy-done.5) | data formatting | bytes 524288 | tf_op jit(solution)/shard_map/reshape | solution.py:532
  165.5 1.8 %reshape.89 = bf16[16,4,2048]{2,1,0:T(4,128)(2,1)} reshape(bf16[64,2048]{1,0:T(8,128)(2,1)} %copy-done.4) | data formatting | bytes 524288 | tf_op jit(solution)/shard_map/reshape | solution.py:531
  (36 shorter events, 0.7 us)
Async XLA Ops:
  0.6 9.6 %copy-start = (bf16[32,32,1024]{2,1,0:T(8,128)(2,1)S(1)}, bf16[32,32,1024]{2,1,0:T(8,128)(2,1)}, u32[]{:S(2)}) copy-start(bf16[32,32,1024]{2,1,0:T(8,128)(2,1)} %param.22) | copy-start | bytes 6291460
  1.6 3.0 %copy-start.10 = (s32[1024]{0:T(1024)}, s32[1024]{0:T(1024)S(1)}, u32[]{:S(2)}) copy-start(s32[1024]{0:T(1024)S(1)} %pad_clamp_fusion.1) | copy-start | bytes 12292
  10.2 2.1 %copy-start.7 = (bf16[2048,16]{0,1:T(8,128)(2,1)S(1)}, bf16[2048,16]{0,1:T(8,128)(2,1)}, u32[]{:S(2)}) copy-start(bf16[2048,16]{0,1:T(8,128)(2,1)} %param.35) | copy-start | bytes 196612
  10.2 2.5 %copy-start.6 = (bf16[16,4,2048]{2,1,0:T(4,128)(2,1)S(1)}, bf16[16,4,2048]{2,1,0:T(4,128)(2,1)}, u32[]{:S(2)}) copy-start(bf16[16,4,2048]{2,1,0:T(4,128)(2,1)} %param.29) | copy-start | bytes 786436
  18.9 0.8 copy-start.3
  65.4 0.7 copy-start.1
  66.1 0.7 copy-start.4
  66.8 4.8 %copy-start.8 = (f32[16,4,32]{2,1,0:T(4,128)S(1)}, f32[16,4,32]{2,1,0:T(4,128)}, u32[]{:S(2)}) copy-start(f32[16,4,32]{2,1,0:T(4,128)} %param.42) | copy-start | bytes 24580
  66.8 4.9 %copy-start.9 = (f32[16,4,32]{2,1,0:T(4,128)S(1)}, f32[16,4,32]{2,1,0:T(4,128)}, u32[]{:S(2)}) copy-start(f32[16,4,32]{2,1,0:T(4,128)} %param.43) | copy-start | bytes 24580
  66.8 4.9 %copy-start.2 = (bf16[64,2176]{1,0:T(8,128)(2,1)S(1)}, bf16[64,2176]{1,0:T(8,128)(2,1)}, u32[]{:S(2)}) copy-start(bf16[64,2176]{1,0:T(8,128)(2,1)} %copy-done.1) | copy-start | bytes 835588
  162.5 1.2 copy-start.5
